TPU v7x, 32 devices: a whole 2x2x4 slice. The times are simulated.
32 devices in a mesh: seq: 16 (over z, y, x), dp: 2 (over core).
Axes of the slice: x: 2, y: 2, z: 4, core: 2. Of those that a mesh axis runs over, the one named last changes fastest.
Arguments:
- tokens: bfloat16 [2, 4096, 1472], P('dp', 'seq'), may hold values from -6 to 6
- cotangent: bfloat16 [2, 4096, 1472], P('dp', 'seq'), may hold values from -6 to 6
- item_lengths: int32 [2, 8], P('dp'), may hold values from 1 to 4, 16 in all within a row
- gain_attn: float32 [1472], replicated, may hold values from 0.1 to 1.9
- gain_ffn: float32 [1472], replicated, may hold values from 0.1 to 1.9
- rel_table: float32 [32, 6], replicated, may hold values from -4 to 4
- w_query: bfloat16 [1472, 384], replicated, may hold values from -0.0546875 to 0.0546875
- w_keyval: bfloat16 [1472, 768], replicated, may hold values from -0.15625 to 0.15625
- w_out: bfloat16 [384, 1472], replicated, may hold values from -1.25 to 1.25
- w_gateup: bfloat16 [1472, 7168], replicated, may hold values from -0.15625 to 0.15625
- w_down: bfloat16 [3584, 1472], replicated, may hold values from -0.09375 to 0.09375
Outputs:
- output: bfloat16 [2, 4096, 1472], P('dp', 'seq')
- input_grad: bfloat16 [2, 4096, 1472], P('dp', 'seq')
- gain_attn_grad: float32 [1472], replicated
- gain_ffn_grad: float32 [1472], replicated
- table_grad: float32 [32, 6], replicated
- query_grad: float32 [1472, 384], P('dp', 'seq')
- keyval_grad: float32 [1472, 768], P('dp', 'seq')
- out_grad: float32 [384, 1472], P('seq', 'dp')
- gateup_grad: float32 [1472, 7168], P('dp', 'seq')
- down_grad: float32 [3584, 1472], P('seq', 'dp')
Inputs may be any that keep to these rules, and one draw needn't show every extreme that they name: `item_lengths`: each group's items fill its 16 blocks end to end; the longest has exactly 4 blocks.
All inputs are finite; a program needn't handle non-finite values.
Results may differ from a plain program's by a relative error of at most 0.015.
The roundings to bfloat16 on the way count: a program that leaves them out, or rounds other values in their place, can miss the bound.
Values may be sent and summed in bfloat16 or wider, within the bound.
No kernel may reach another device: no remote copies, remote signals or barrier semaphores. Data moves between devices by JAX's collectives and lax.ppermute only.
A program may use at most 256 MiB of HBM per device.

v0:
```python
import functools

import jax
import jax.numpy as jnp
from jax import lax
from jax.experimental import pallas as pl
from jax.experimental.pallas import tpu as pltpu
from jax.sharding import PartitionSpec as P

H = 6
DH = 64
BUCKETS = 32
ITEM_MOST = 4
REACH = ITEM_MOST - 1
PAIR = 2 * DH
UNITS = 896

bucket_edges = (12, 16, 23, 32, 46, 64, 91)
negative_fill = -1e30
f32 = jnp.float32
bf16 = jnp.bfloat16
VMEM_MOST = 56 * 1024 * 1024
FLOPS_PER_US = 5_000_000_000


def bucket_of(relative):
    ahead = jnp.where(relative > 0, 16, 0).astype(jnp.int32)
    distance = jnp.abs(relative)
    beyond = 8 + sum(((distance >= edge).astype(jnp.int32) for edge in bucket_edges))
    return ahead + jnp.where(distance < 8, distance, beyond)


def dot_nn(left, right):
    return lax.dot_general(left, right, (((1,), (0,)), ((), ())), preferred_element_type=f32)


def dot_nt(left, right):
    return lax.dot_general(left, right, (((1,), (1,)), ((), ())), preferred_element_type=f32)


def dot_tn(left, right):
    return lax.dot_general(left, right, (((0,), (0,)), ((), ())), preferred_element_type=f32)


def rms_scale(values):
    return lax.rsqrt(jnp.mean(values * values, axis=-1, keepdims=True) + 1e-06)


def lasting(microseconds):
    return pl.CostEstimate(
        flops=int(microseconds * FLOPS_PER_US), bytes_accessed=0, transcendentals=0
    )


def whole(shape):
    return pl.BlockSpec(shape, lambda *_: (0,) * len(shape))


def params():
    return pltpu.CompilerParams(vmem_limit_bytes=VMEM_MOST)


def up_to(count, step):
    return -(-count // step) * step


def spread_width(width):
    return 2 * up_to(width // 2, 128)


def spread_rows(out, value, gain=None):
    half = value.shape[0] // 2
    each = out.shape[1] // 2
    nothing = jnp.zeros((out.shape[0], each - half), out.dtype)
    for index in range(2):
        part = value[index * half : (index + 1) * half].T
        if gain is not None:
            part = part * gain[:, index * half : (index + 1) * half]
        out[:, index * each : index * each + half] = part.astype(out.dtype)
        out[:, index * each + half : (index + 1) * each] = nothing


def spread_depth(value, wide):
    half = value.shape[0] // 2
    nothing = jnp.zeros((wide // 2 - half, value.shape[1]), value.dtype)
    return jnp.concatenate([value[:half], nothing, value[half:], nothing], 0)


def as_column(row):
    return jnp.broadcast_to(row, (128, row.shape[1])).T[:, :1]


def as_row(column):
    return jnp.broadcast_to(column, (column.shape[0], 128)).T[:1]


def shift_by_head(value):
    return pltpu.roll(value, DH, 1)


def columns(value, index):
    return value[:, index * PAIR : (index + 1) * PAIR]


def low_lanes(shape):
    return lax.broadcasted_iota(jnp.int32, shape, len(shape) - 1) % PAIR < DH


def packed_heads(query, keyval, half):
    low = low_lanes((query.shape[0], PAIR))
    key = [columns(keyval, i) for i in range(3)]
    value = [columns(keyval, i + 3) for i in range(3)]
    ask = [columns(query, i) for i in range(3)]
    if half == 0:
        parts = [
            key[0],
            jnp.where(low, key[1], shift_by_head(value[1])),
            value[0],
            ask[0],
            jnp.where(low, ask[1], 0.0),
        ]
    else:
        parts = [
            key[2],
            jnp.where(low, shift_by_head(key[1]), value[1]),
            value[2],
            ask[2],
            jnp.where(low, shift_by_head(ask[1]), 0.0),
        ]
    return jnp.concatenate(parts, 1).astype(bf16)


def open_kernel(
    spot_ref, inputs_ref, gain_ref, w_query_ref, w_keyval_ref, hidden_ref, mine_ref, other_ref
):
    inputs = inputs_ref[...].astype(f32)
    scale = lax.rsqrt(jnp.mean(inputs * inputs, axis=0, keepdims=True) + 1e-06)
    spread_rows(hidden_ref, inputs * scale, gain_ref[...])
    hidden = hidden_ref[...]
    wide = hidden.shape[1]
    keyval = dot_nn(hidden, spread_depth(w_keyval_ref[...], wide))
    query = dot_nn(hidden, spread_depth(w_query_ref[...], wide))
    first = packed_heads(query, keyval, 0)
    second = packed_heads(query, keyval, 1)

    @pl.when(spot_ref[0] == 0)
    def _():
        mine_ref[...] = first
        other_ref[...] = second

    @pl.when(spot_ref[0] != 0)
    def _():
        mine_ref[...] = second
        other_ref[...] = first


def opened(spot, inputs, gain, w_query, w_keyval):
    width, rows = inputs.shape
    inner = w_query.shape[1]
    pack = jax.ShapeDtypeStruct((rows, 5 * PAIR), bf16)
    return pl.pallas_call(
        open_kernel,
        grid_spec=pltpu.PrefetchScalarGridSpec(
            num_scalar_prefetch=1,
            grid=(1,),
            in_specs=[
                whole((width, rows)),
                whole((1, width)),
                whole((width, inner)),
                whole((width, 2 * inner)),
            ],
            out_specs=[
                whole((rows, spread_width(width))),
                whole(pack.shape),
                whole(pack.shape),
            ],
        ),
        out_shape=[jax.ShapeDtypeStruct((rows, spread_width(width)), bf16), pack, pack],
        compiler_params=params(),
        cost_estimate=lasting(5),
    )(spot, inputs, gain, w_query, w_keyval)


def turn_kernel(in_ref, out_ref):
    spread_rows(out_ref, in_ref[...])


def turned_rows(value):
    width, rows = value.shape
    return pl.pallas_call(
        turn_kernel,
        out_shape=jax.ShapeDtypeStruct((rows, spread_width(width)), value.dtype),
        compiler_params=params(),
        cost_estimate=lasting(2),
    )(value)


def bias_kernel(place_ref, by_shift_ref, out_ref):
    rows, keys = out_ref.shape[2:]
    wide = by_shift_ref.shape[-1]
    spread = jnp.broadcast_to(by_shift_ref[0, 0], (rows, wide))
    turned = pltpu.roll(spread, 0, 1, stride=1, stride_axis=0)[:, :keys]
    key = lax.broadcasted_iota(jnp.int32, (rows, keys), 1)
    length = place_ref[2 + pl.program_id(0)]
    out_ref[0, 0] = jnp.where(key < length * rows, turned, negative_fill)


def window_bias(place, by_shift, rows):
    keys = ITEM_MOST * rows
    both, heads, wide = by_shift.shape
    return pl.pallas_call(
        bias_kernel,
        grid_spec=pltpu.PrefetchScalarGridSpec(
            num_scalar_prefetch=1,
            grid=(both, heads),
            in_specs=[pl.BlockSpec((1, 1, 1, wide), lambda b, h, _: (b, h, 0, 0))],
            out_specs=pl.BlockSpec((1, 1, rows, keys), lambda b, h, _: (b, h, 0, 0)),
        ),
        out_shape=jax.ShapeDtypeStruct((both, heads, rows, keys), f32),
        compiler_params=params(),
        cost_estimate=lasting(6),
    )(place, by_shift.reshape(both, heads, 1, wide))


SLOTS = 2 * REACH + 2


def pair_kernel(spot_ref, mine_ref, got_ref, both_ref, first_ref, second_ref):
    rows = mine_ref.shape[0]
    wide = first_ref.shape[1]
    mine, got = mine_ref[:, :wide], got_ref[:, :wide]

    def put(first, second):
        first_ref[...] = first
        second_ref[...] = second
        both_ref[:rows, :] = first
        both_ref[rows:, :] = second

    @pl.when(spot_ref[0] == 0)
    def _():
        put(mine, got)

    @pl.when(spot_ref[0] != 0)
    def _():
        put(got, mine)


def paired(spot, mine, got):
    rows = mine.shape[0]
    shapes = [(2 * rows, 3 * PAIR), (rows, 3 * PAIR), (rows, 3 * PAIR)]
    return pl.pallas_call(
        pair_kernel,
        grid_spec=pltpu.PrefetchScalarGridSpec(
            num_scalar_prefetch=1,
            grid=(1,),
            in_specs=[whole(mine.shape)] * 2,
            out_specs=[whole(shape) for shape in shapes],
        ),
        out_shape=[jax.ShapeDtypeStruct(shape, bf16) for shape in shapes],
        compiler_params=params(),
        cost_estimate=lasting(1),
    )(spot, mine, got)


GROUPS = ((0, 2), (0, 2), (1, 1))


def spread_heads(own, mine, got):
    value = jnp.where(own, mine, got)
    first = columns(value, 0)
    low = low_lanes(first.shape)
    nothing = jnp.zeros_like(first)
    return jnp.where(low, first, nothing), jnp.where(low, nothing, first), columns(value, 1)


def attend_kernel(
    place_ref, mine_ref, got_ref, behind_far, behind, pair_ref, ahead, ahead_far, bias_ref,
    attended_mine, attended_other, prob_ref, window_ref
):
    rows = mine_ref.shape[0]
    wide = window_ref.shape[1]
    block = pl.program_id(0)
    own = block == place_ref[4]

    @pl.when(block == 0)
    def _():
        at = 0
        for piece in (behind_far, behind, pair_ref, ahead, ahead_far):
            window_ref[at : at + piece.shape[0], :] = piece[...]
            at += piece.shape[0]

    asks = spread_heads(own, mine_ref[:, wide:], got_ref[:, wide:])
    start = pl.multiple_of((REACH + block - place_ref[block]) * rows, rows)
    window = window_ref[pl.ds(start, ITEM_MOST * rows), :]
    parts = []
    for head, (key, value) in enumerate(GROUPS):
        scores = dot_nt(asks[head], columns(window, key)) + bias_ref[0, head]
        exponent = jnp.exp(scores - jnp.max(scores, axis=-1, keepdims=True))
        prob = exponent / jnp.sum(exponent, axis=-1, keepdims=True)
        prob_ref[0, head] = prob
        parts.append(dot_nn(prob.astype(bf16), columns(window, value)))

    def put(out):
        low = low_lanes((rows, PAIR))
        out[:PAIR, :] = jnp.where(low, parts[0], parts[1]).T.astype(bf16)
        out[PAIR:, :] = parts[2].T[DH:].astype(bf16)

    @pl.when(own)
    def _():
        put(attended_mine)

    @pl.when(jnp.logical_not(own))
    def _():
        put(attended_other)


def attend(place, mine, got, pieces, bias):
    rows = mine.shape[0]
    keys = ITEM_MOST * rows
    wide = pieces[0].shape[1]
    heads = bias.shape[1]
    tall = pl.BlockSpec((1, heads, rows, keys), lambda b, _: (b, 0, 0, 0))
    return pl.pallas_call(
        attend_kernel,
        grid_spec=pltpu.PrefetchScalarGridSpec(
            num_scalar_prefetch=1,
            grid=(2,),
            in_specs=[whole(mine.shape)] * 2 + [whole(piece.shape) for piece in pieces] + [tall],
            out_specs=[
                whole((heads * DH, rows)),
                whole((heads * DH, rows)),
                tall,
                whole((SLOTS * rows, wide)),
            ],
        ),
        out_shape=[
            jax.ShapeDtypeStruct((heads * DH, rows), bf16),
            jax.ShapeDtypeStruct((heads * DH, rows), bf16),
            jax.ShapeDtypeStruct((2, heads, rows, keys), f32),
            jax.ShapeDtypeStruct((SLOTS * rows, wide), bf16),
        ],
        compiler_params=params(),
        cost_estimate=lasting(9),
    )(place, mine, got, *pieces, bias)


def natural_heads(half, mine, other, out):
    each = mine.shape[0]

    def put(first, second):
        out[:each, :] = first[...]
        out[each : each + DH, :] = second[PAIR:, :]
        out[each + DH :, :] = second[:PAIR, :]

    @pl.when(half == 0)
    def _():
        put(mine, other)

    @pl.when(half != 0)
    def _():
        put(other, mine)


def middle_kernel(
    spot_ref, mine_ref, other_ref, inputs_ref, w_out_ref, gain_ref, middle_ref, hidden_ref, attended
):
    natural_heads(spot_ref[0], mine_ref, other_ref, attended)
    middle = inputs_ref[...].astype(f32) + dot_nn(w_out_ref[...], attended[...])
    middle_ref[...] = middle
    scale = lax.rsqrt(jnp.mean(middle * middle, axis=0, keepdims=True) + 1e-06)
    spread_rows(hidden_ref, middle * scale, gain_ref[...])


def middle_part(spot, mine, other, inputs, w_out, gain):
    width, rows = inputs.shape
    inner = w_out.shape[1]
    return pl.pallas_call(
        middle_kernel,
        grid_spec=pltpu.PrefetchScalarGridSpec(
            num_scalar_prefetch=1,
            grid=(1,),
            in_specs=[
                whole(mine.shape),
                whole(other.shape),
                whole((width, rows)),
                whole((width, inner)),
                whole((1, width)),
            ],
            out_specs=[whole((width, rows)), whole((rows, spread_width(width)))],
            scratch_shapes=[pltpu.VMEM((inner, rows), bf16)],
        ),
        out_shape=[
            jax.ShapeDtypeStruct((width, rows), f32),
            jax.ShapeDtypeStruct((rows, spread_width(width)), bf16),
        ],
        compiler_params=params(),
        cost_estimate=lasting(4),
    )(spot, mine, other, inputs, w_out, gain)


GELU_A = 0.7978845608028654
GELU_B = 0.044715


def packed_back(back, half):
    low = low_lanes((back.shape[0], PAIR))
    middle = columns(back, 1)
    if half == 0:
        parts = [columns(back, 0), jnp.where(low, 0.0, shift_by_head(middle))]
    else:
        parts = [columns(back, 2), jnp.where(low, 0.0, middle)]
    return jnp.concatenate(parts, 1).astype(bf16)


def ffn_kernel(last, spot_ref, hidden_ref, upstream_ref, gate_w_ref, up_w_ref, down_w_ref, *refs):
    if last:
        out_in, back_in, middle_ref, gain_ref, w_out_ref, cotangent_ref = refs[:6]
        (mixed_ref, both_ref, output_ref, gain_grad_ref, middle_back_ref,
         branch_ref, back_mine_ref, back_other_ref, out_ref, back_ref) = refs[6:]
    else:
        mixed_ref, both_ref, out_ref, back_ref = refs
    step = pl.program_id(0)
    units = gate_w_ref.shape[1]
    hidden = hidden_ref[...]
    wide = hidden.shape[1]
    upstream = upstream_ref[...]
    gateup_w = jnp.concatenate([gate_w_ref[...], up_w_ref[...]], 1)
    gateup = dot_nn(hidden, spread_depth(gateup_w, wide))
    gate, up = gateup[:, :units], gateup[:, units:]
    mixed_back = dot_nn(upstream, spread_depth(down_w_ref[...], wide))
    squared = gate * gate
    bent = jnp.tanh(GELU_A * (gate + GELU_B * (squared * gate)))
    share = 0.5 * (1.0 + bent)
    gelu = gate * share
    slope = share + 0.5 * gate * (1.0 - bent * bent) * (GELU_A * (1.0 + 3.0 * GELU_B * squared))
    mixed = (gelu * up).astype(bf16).T
    gate_back = (mixed_back * up * slope).astype(bf16).T
    up_back = (mixed_back * gelu).astype(bf16).T
    mixed_ref[...] = mixed
    both_ref[0] = gate_back
    both_ref[1] = up_back
    forward = dot_nn(down_w_ref[...], mixed)
    backward = dot_nn(gateup_w, jnp.concatenate([gate_back, up_back], 0))

    @pl.when(step == 0)
    def _():
        if last:
            out_ref[...] = out_in[...] + forward
            back_ref[...] = back_in[...] + backward
        else:
            out_ref[...] = forward
            back_ref[...] = backward

    @pl.when(step > 0)
    def _():
        out_ref[...] += forward
        back_ref[...] += backward

    if not last:
        return

    @pl.when(step == pl.num_programs(0) - 1)
    def _():
        middle = middle_ref[...]
        output_ref[...] = (middle + out_ref[...]).astype(bf16)
        scale = lax.rsqrt(jnp.mean(middle * middle, axis=0, keepdims=True) + 1e-06)
        normed = middle * scale
        back = back_ref[...]
        gain_grad_ref[...] = as_row(jnp.sum(back * normed, axis=1, keepdims=True))
        normed_back = back * as_column(gain_ref[...])
        mean = jnp.mean(normed_back * normed, axis=0, keepdims=True)
        middle_back = cotangent_ref[...].astype(f32) + scale * (normed_back - normed * mean)
        middle_back_ref[...] = middle_back
        spread_rows(branch_ref, middle_back)
        attended_back = dot_nn(branch_ref[...], spread_depth(w_out_ref[...], wide))
        first = packed_back(attended_back, 0)
        second = packed_back(attended_back, 1)

        @pl.when(spot_ref[0] == 0)
        def _():
            back_mine_ref[...] = first
            back_other_ref[...] = second

        @pl.when(spot_ref[0] != 0)
        def _():
            back_mine_ref[...] = second
            back_other_ref[...] = first


def ffn_half(last, spot, hidden, upstream, w_gateup, w_down, more=()):
    rows, wide = hidden.shape
    width, units = w_down.shape
    steps = units // 2 // UNITS
    both = units // UNITS
    in_specs = [
        whole((rows, wide)),
        whole((rows, wide)),
        pl.BlockSpec((width, UNITS), lambda j, s: (0, s[1] * steps + j)),
        pl.BlockSpec((width, UNITS), lambda j, s: (0, both + s[1] * steps + j)),
        pl.BlockSpec((width, UNITS), lambda j, s: (0, s[1] * steps + j)),
    ] + [whole(value.shape) for value in more]
    sums = [jax.ShapeDtypeStruct((width, rows), f32)] * 2
    out_specs = [
        pl.BlockSpec((UNITS, rows), lambda j, s: (j, 0)),
        pl.BlockSpec((2, UNITS, rows), lambda j, s: (0, j, 0)),
    ]
    out_shape = [
        jax.ShapeDtypeStruct((units // 2, rows), bf16),
        jax.ShapeDtypeStruct((2, units // 2, rows), bf16),
    ]
    if last:
        rest = [
            jax.ShapeDtypeStruct((width, rows), bf16),
            jax.ShapeDtypeStruct((1, width), f32),
            jax.ShapeDtypeStruct((width, rows), f32),
            jax.ShapeDtypeStruct((rows, wide), bf16),
            jax.ShapeDtypeStruct((rows, 2 * PAIR), bf16),
            jax.ShapeDtypeStruct((rows, 2 * PAIR), bf16),
        ]
    else:
        rest = sums
    return pl.pallas_call(
        functools.partial(ffn_kernel, last),
        grid_spec=pltpu.PrefetchScalarGridSpec(
            num_scalar_prefetch=1,
            grid=(steps,),
            in_specs=in_specs,
            out_specs=out_specs + [whole(value.shape) for value in rest],
            scratch_shapes=[pltpu.VMEM((width, rows), f32)] * 2 if last else [],
        ),
        out_shape=out_shape + rest,
        compiler_params=params(),
        cost_estimate=lasting(20),
    )(spot, hidden, upstream, w_gateup, w_gateup, w_down, *more)


def half_of(ref, index):
    each = ref.shape[1] // 2
    return ref[:, pl.ds(pl.multiple_of(index * each, 128), each)]


def pair_grad_kernel(
    parts, spot_ref, left_own, left_other, left_far, right_own, right_far, *refs
):
    outs, halves = refs[:-1], refs[-1]
    rows = left_far.shape[-1]
    mine = spot_ref[0]

    @pl.when(pl.program_id(0) == 0)
    def _():
        for index, right in enumerate((right_own, right_far)):
            at = slice(index * rows, (index + 1) * rows)
            halves[0, at, :] = half_of(right, mine)
            halves[1, at, :] = half_of(right, 1 - mine)

    own = left_own[0] if left_other is None else jnp.where(spot_ref[1] != 0, left_own[0], left_other[0])
    left = jnp.concatenate([own, left_far[0]], 1)
    each = left.shape[0] // parts
    for half in range(2):
        product = dot_nn(left, halves[half]).astype(bf16)
        for part in range(parts):
            outs[2 * part + half][...] = product[part * each : (part + 1) * each]


def pair_grad(spot, tiles, tile, parts, left_own, left_far, right_own, right_far):
    count, place = tiles
    rows = left_far.shape[-1]
    wide = right_own.shape[1] // 2
    each = tile // parts
    out = jax.ShapeDtypeStruct((count * each, wide), bf16)
    left = pl.BlockSpec((1, tile, rows), lambda j, _: (*place(j), 0))

    def kernel(spot_ref, *refs):
        if len(left_own) == 1:
            pair_grad_kernel(parts, spot_ref, refs[0], None, *refs[1:])
        else:
            pair_grad_kernel(parts, spot_ref, *refs)

    return pl.pallas_call(
        kernel,
        grid_spec=pltpu.PrefetchScalarGridSpec(
            num_scalar_prefetch=1,
            grid=(count,),
            in_specs=[left] * (len(left_own) + 1) + [whole(right_own.shape), whole(right_far.shape)],
            out_specs=[pl.BlockSpec((each, wide), lambda j, _: (j, 0))] * (2 * parts),
            scratch_shapes=[pltpu.VMEM((2, 2 * rows, wide), bf16)],
        ),
        out_shape=[out] * (2 * parts),
        compiler_params=params(),
        cost_estimate=lasting(24),
    )(spot, *left_own, left_far, right_own, right_far)


def quad_grad_kernel(
    parts, spot_ref, left_own, left_far, left_own_got, left_far_got, *refs
):
    rights, outs, halves = refs[:4], refs[4:-1], refs[-1]
    rows = left_own.shape[-1]
    mine = spot_ref[0]

    @pl.when((pl.program_id(0) == 0) & (pl.program_id(1) == 0))
    def _():
        for index, right in enumerate(rights):
            at = slice(index * rows, (index + 1) * rows)
            halves[0, at, :] = half_of(right, mine)
            halves[1, at, :] = half_of(right, 1 - mine)

    left = jnp.concatenate([left_own[0], left_far[0], left_own_got[0], left_far_got[0]], 1)
    each = left.shape[0] // parts
    for half in range(2):
        product = dot_nn(left, halves[half]).astype(bf16)
        for part in range(parts):
            outs[2 * part + half][...] = product[part * each : (part + 1) * each]


def quad_grad(spot, owned, parts, lefts, lefts_got, rights):
    groups, units, rows = lefts_got[0].shape
    wide = rights[0].shape[1] // 2
    runs = units // owned
    each = owned // parts
    out = jax.ShapeDtypeStruct((groups * runs * each, wide), bf16)
    return pl.pallas_call(
        functools.partial(quad_grad_kernel, parts),
        grid_spec=pltpu.PrefetchScalarGridSpec(
            num_scalar_prefetch=1,
            grid=(groups, runs),
            in_specs=[pl.BlockSpec((1, owned, rows), lambda g, j, s: (g, 2 * j + s[1], 0))] * 2
            + [pl.BlockSpec((1, owned, rows), lambda g, j, s: (g, j, 0))] * 2
            + [whole(right.shape) for right in rights],
            out_specs=[pl.BlockSpec((each, wide), lambda g, j, s: (g * runs + j, 0))] * (2 * parts),
            scratch_shapes=[pltpu.VMEM((2, 4 * rows, wide), bf16)],
        ),
        out_shape=[out] * (2 * parts),
        compiler_params=params(),
        cost_estimate=lasting(12),
    )(spot, *lefts, *lefts_got, *rights)


def heads_grad_kernel(
    spot_ref, keyval_ref, query_ref, attended_own, attended_far, hidden_own, hidden_far, branch_own,
    branch_far, kept_ref, sent_ref, low, high, left
):
    rows = hidden_own.shape[0]
    mine, half = spot_ref[0], spot_ref[1]
    each = query_ref.shape[1]

    def ordered(source, at, first, second):
        @pl.when(half == 0)
        def _():
            for start, stop, to in first:
                left[at + to : at + to + stop - start, :] = source(start, stop)

        @pl.when(half != 0)
        def _():
            for start, stop, to in second:
                left[at + to : at + to + stop - start, :] = source(start, stop)

    same = ((0, 3 * DH, 0),)
    turned = ((PAIR, 3 * DH, 0), (0, PAIR, DH))
    value_first = ((4 * DH, 6 * DH, 0), (3 * DH, 4 * DH, PAIR))
    value_second = ((3 * DH, 6 * DH, 0),)

    def joined(ref):
        return lambda start, stop: jnp.concatenate(
            [ref[0, start:stop, :], ref[1, start:stop, :]], 1
        )

    def plain(start, stop):
        return keyval_ref[start:stop, :]

    ordered(joined(query_ref), 0, same, turned)
    ordered(plain, each, same, turned)
    ordered(plain, 2 * each, value_first, value_second)

    def by_side(start, stop):
        own, far = attended_own[start:stop, :], attended_far[start:stop, :]
        first = jnp.where(half == 0, own, far)
        second = jnp.where(half == 0, far, own)
        return jnp.concatenate([first, second], 1)

    ordered(by_side, 3 * each, same, turned)
    for own, far, at, stop in (
        (hidden_own, hidden_far, 0, 3 * each),
        (branch_own, branch_far, 3 * each, 4 * each),
    ):
        for index, source in ((0, own), (1, far)):

            @pl.when(half == index)
            def _():
                low[:rows, :] = half_of(source, mine)
                high[:rows, :] = half_of(source, 1 - mine)

            @pl.when(half != index)
            def _():
                low[rows:, :] = half_of(source, mine)
                high[rows:, :] = half_of(source, 1 - mine)

        kept_ref[at:stop, :] = dot_nn(left[at:stop, :], low[...]).astype(bf16)
        sent_ref[at:stop, :] = dot_nn(left[at:stop, :], high[...]).astype(bf16)


def heads_grad(spot, keyval, query, attended, hiddens, branches):
    wide = hiddens[0].shape[1] // 2
    rows = hiddens[0].shape[0]
    each = query.shape[1]
    out = jax.ShapeDtypeStruct((4 * each, wide), bf16)
    operands = (keyval, query, *attended, *hiddens, *branches)
    return pl.pallas_call(
        heads_grad_kernel,
        grid_spec=pltpu.PrefetchScalarGridSpec(
            num_scalar_prefetch=1,
            grid=(1,),
            in_specs=[whole(value.shape) for value in operands],
            out_specs=[whole(out.shape)] * 2,
            scratch_shapes=[pltpu.VMEM((2 * rows, wide), bf16)] * 2
            + [pltpu.VMEM((4 * each, 2 * rows), bf16)],
        ),
        out_shape=[out, out],
        compiler_params=params(),
        cost_estimate=lasting(2.1),
    )(spot, *operands)


def attend_back_kernel(
    place_ref, mine_ref, got_ref, window_ref, prob_ref, back_mine, back_got, query_back_ref,
    by_shift_ref, behind_far, behind, pair_ref, ahead, ahead_far, total
):
    rows = mine_ref.shape[0]
    wide = window_ref.shape[1]
    keys = ITEM_MOST * rows
    block = pl.program_id(0)
    own = block == place_ref[4]
    asks = spread_heads(own, mine_ref[:, wide:], got_ref[:, wide:])
    backs = spread_heads(own, back_mine[...], back_got[...])

    @pl.when(block == 0)
    def _():
        total[...] = jnp.zeros_like(total)

    start = pl.multiple_of((REACH + block - place_ref[block]) * rows, rows)
    window = window_ref[pl.ds(start, keys), :]
    row = lax.broadcasted_iota(jnp.int32, (rows, rows), 0)
    column = lax.broadcasted_iota(jnp.int32, (rows, rows), 1)
    flip = jnp.where(row + column == rows - 1, 1.0, 0.0).astype(bf16)
    parts, sums = [], [None] * 3
    for head, (key, value) in enumerate(GROUPS):
        prob = prob_ref[0, head]
        prob_back = dot_nt(backs[head], columns(window, value))
        delta = jnp.sum(prob * prob_back, axis=-1, keepdims=True)
        score_back = (prob * (prob_back - delta)).astype(bf16)
        parts.append(dot_nn(score_back, columns(window, key)))
        key_part = dot_tn(asks[head], score_back)
        value_part = dot_tn(backs[head], prob.astype(bf16))
        for group, add in ((key, key_part), (value, value_part)):
            sums[group] = add if sums[group] is None else sums[group] + add
        flipped = jnp.concatenate([dot_nn(flip, score_back), jnp.zeros((rows, rows), f32)], 1)
        turned = pltpu.roll(flipped, keys + 1, 1, stride=1, stride_axis=0)
        by_shift_ref[0, head] = jnp.sum(turned, axis=0, keepdims=True)
    low = low_lanes((rows, PAIR))
    query_back_ref[0, :PAIR, :] = jnp.where(low, parts[0], parts[1]).T.astype(bf16)
    query_back_ref[0, PAIR:, :] = parts[2].T[:DH].astype(bf16)
    for group in range(3):
        total[group * PAIR : (group + 1) * PAIR, pl.ds(start, keys)] += sums[group]

    @pl.when(block == 1)
    def _():
        at = 0
        for out in (behind_far, behind, pair_ref, ahead, ahead_far):
            out[...] = total[:, at : at + out.shape[1]].astype(out.dtype)
            at += out.shape[1]


def attend_back(place, mine, got, window, prob, back_mine, back_got):
    rows = mine.shape[0]
    _, heads, _, keys = prob.shape
    wide = window.shape[1]
    pieces = [(rows, bf16), (2 * rows, bf16), (2 * rows, f32), (2 * rows, bf16), (rows, bf16)]
    return pl.pallas_call(
        attend_back_kernel,
        grid_spec=pltpu.PrefetchScalarGridSpec(
            num_scalar_prefetch=1,
            grid=(2,),
            in_specs=[
                whole(mine.shape),
                whole(got.shape),
                whole(window.shape),
                pl.BlockSpec((1, heads, rows, keys), lambda b, _: (b, 0, 0, 0)),
                whole(back_mine.shape),
                whole(back_got.shape),
            ],
            out_specs=[
                pl.BlockSpec((1, heads * DH, rows), lambda b, _: (b, 0, 0)),
                pl.BlockSpec((1, heads, 1, keys + rows), lambda b, _: (b, 0, 0, 0)),
            ]
            + [whole((wide, count)) for count, _ in pieces],
            scratch_shapes=[
                pltpu.VMEM((wide, SLOTS * rows), f32),
            ],
        ),
        out_shape=[
            jax.ShapeDtypeStruct((2, heads * DH, rows), bf16),
            jax.ShapeDtypeStruct((2, heads, 1, keys + rows), f32),
        ]
        + [jax.ShapeDtypeStruct((wide, count), dtype) for count, dtype in pieces],
        compiler_params=params(),
        cost_estimate=lasting(3.6),
    )(place, mine, got, window, prob, back_mine, back_got)


def gather_kernel(
    spot_ref, pair_ref, behind, ahead, behind_far, ahead_far, query_ref, both_ref, mine_ref,
    other_ref
):
    rows = behind_far.shape[1]
    wide = pair_ref.shape[0]
    total = pair_ref[...] + behind[...].astype(f32) + ahead[...].astype(f32)
    first = (total[:, :rows] + behind_far[...].astype(f32)).astype(bf16)
    second = (total[:, rows:] + ahead_far[...].astype(f32)).astype(bf16)
    both_ref[:, :rows] = first
    both_ref[:, rows:] = second

    @pl.when(spot_ref[0] == 0)
    def _():
        mine_ref[:wide, :] = first
        other_ref[:wide, :] = second
        mine_ref[wide:, :] = query_ref[0]
        other_ref[wide:, :] = query_ref[1]

    @pl.when(spot_ref[0] != 0)
    def _():
        mine_ref[:wide, :] = second
        other_ref[:wide, :] = first
        mine_ref[wide:, :] = query_ref[1]
        other_ref[wide:, :] = query_ref[0]


def gathered(spot, pair, behind, ahead, behind_far, ahead_far, query):
    wide, rows = behind_far.shape
    operands = (pair, behind, ahead, behind_far, ahead_far, query)
    pack = jax.ShapeDtypeStruct((wide + query.shape[1], rows), bf16)
    both = jax.ShapeDtypeStruct((wide, 2 * rows), bf16)
    return pl.pallas_call(
        gather_kernel,
        grid_spec=pltpu.PrefetchScalarGridSpec(
            num_scalar_prefetch=1,
            grid=(1,),
            in_specs=[whole(value.shape) for value in operands],
            out_specs=[whole(both.shape), whole(pack.shape), whole(pack.shape)],
        ),
        out_shape=[both, pack, pack],
        compiler_params=params(),
        cost_estimate=lasting(3),
    )(spot, *operands)


def close_kernel(
    spot_ref, mine_ref, other_ref, inputs_ref, middle_back_ref, w_query_ref, w_keyval_ref,
    gain_ref, input_back_ref, gain_grad_ref, query_back, keyval_back
):
    inner = query_back.shape[0]
    each = inner // 2

    def put(first, second):
        keyval_back[:each, :] = first[:each, :]
        keyval_back[each : each + DH, :] = second[PAIR : PAIR + DH, :]
        keyval_back[each + DH : inner, :] = second[:PAIR, :]
        keyval_back[inner : inner + PAIR, :] = first[4 * DH : 6 * DH, :]
        keyval_back[inner + PAIR : inner + each, :] = first[3 * DH : 4 * DH, :]
        keyval_back[inner + each :, :] = second[3 * DH : 6 * DH, :]
        query_back[:each, :] = first[inner:, :]
        query_back[each : each + DH, :] = second[inner + PAIR :, :]
        query_back[each + DH :, :] = second[inner : inner + PAIR, :]

    @pl.when(spot_ref[0] == 0)
    def _():
        put(mine_ref, other_ref)

    @pl.when(spot_ref[0] != 0)
    def _():
        put(other_ref, mine_ref)

    inputs = inputs_ref[...].astype(f32)
    scale = lax.rsqrt(jnp.mean(inputs * inputs, axis=0, keepdims=True) + 1e-06)
    normed = inputs * scale
    back = dot_nn(w_query_ref[...], query_back[...]) + dot_nn(w_keyval_ref[...], keyval_back[...])
    gain_grad_ref[...] = as_row(jnp.sum(back * normed, axis=1, keepdims=True))
    normed_back = back * as_column(gain_ref[...])
    mean = jnp.mean(normed_back * normed, axis=0, keepdims=True)
    input_back_ref[...] = (
        middle_back_ref[...] + scale * (normed_back - normed * mean)
    ).astype(bf16)


def closed(spot, mine, other, inputs, middle_back, w_query, w_keyval, gain):
    width, rows = inputs.shape
    inner = w_query.shape[1]
    operands = (mine, other, inputs, middle_back, w_query, w_keyval, gain)
    return pl.pallas_call(
        close_kernel,
        grid_spec=pltpu.PrefetchScalarGridSpec(
            num_scalar_prefetch=1,
            grid=(1,),
            in_specs=[whole(value.shape) for value in operands],
            out_specs=[whole((width, rows)), whole((1, width))],
            scratch_shapes=[
                pltpu.VMEM((inner, rows), bf16),
                pltpu.VMEM((2 * inner, rows), bf16),
            ],
        ),
        out_shape=[
            jax.ShapeDtypeStruct((width, rows), bf16),
            jax.ShapeDtypeStruct((1, width), f32),
        ],
        compiler_params=params(),
        cost_estimate=lasting(18),
    )(spot, *operands)


def swapped(value, axis, bit):
    size = lax.axis_size(axis)
    return lax.ppermute(value, axis, [(i, i ^ bit) for i in range(size)])


def passed_along(value, axis, by):
    size = lax.axis_size(axis)
    pairs = [(i, i + by) for i in range(size) if 0 <= i + by < size]
    return lax.ppermute(value, axis, pairs)


def of_both(value, bit):
    size = lax.axis_size("seq")
    groups = [[i, i | bit] for i in range(size) if not i & bit]
    return lax.all_gather(value, "seq", axis=0, tiled=True, axis_index_groups=groups)


def chosen(value, dim, index):
    return lax.dynamic_index_in_dim(value, index, dim, keepdims=False)


def added(left, right):
    return (left.astype(f32) + right.astype(f32)).astype(bf16)


def parted(state, dims, bit):
    left, right = state
    dim = dims.index(bit)
    mine = (lax.axis_index("seq") // bit) % 2
    kept = added(chosen(left, dim, mine), chosen(right, dim, mine))
    sent = added(chosen(left, dim, 1 - mine), chosen(right, dim, 1 - mine))
    return kept, sent, dims[:dim] + dims[dim + 1 :]


def after(value, *others):
    return lax.optimization_barrier((value, *others))[0]


class Halving:
    def __init__(self, state, dims, order):
        self.kept, self.got = state
        self.dims, self.order = dims, list(order)

    def step(self, earlier):
        bit = self.order.pop(0)
        got = after(self.got, earlier)
        self.kept, sent, self.dims = parted((self.kept, got), self.dims, bit)
        self.got = swapped(sent, "seq", bit)
        return sent

    def total(self, dtype=bf16):
        return (self.kept.astype(f32) + self.got.astype(f32)).astype(dtype)


def on_device(
    tokens,
    cotangent,
    item_lengths,
    gain_attn,
    gain_ffn,
    rel_table,
    w_query,
    w_keyval,
    w_out,
    w_gateup,
    w_down,
):
    rows = tokens.shape[1]
    width = tokens.shape[2]
    part = width // 2
    inner = w_query.shape[1]
    blocks = lax.axis_size("seq")
    me = lax.axis_index("seq")
    core = lax.axis_index("dp").astype(jnp.int32)
    top, pair, third = blocks // 2, blocks // 4, blocks // 8
    low = [1 << i for i in range(blocks.bit_length() - 1)][:-2]

    inputs = tokens[0].T
    cotangent = cotangent[0].T
    w_out = w_out.T
    w_down = w_down.T
    gain_attn = gain_attn[None]
    gain_ffn = gain_ffn[None]

    def bit_of(bit):
        return ((me // bit) % 2).astype(jnp.int32)

    side = bit_of(1)
    half = bit_of(pair)
    down_half = bit_of(third)

    hidden_one, mine, other = opened(side[None], inputs, gain_attn, w_query, w_keyval)
    got = swapped(other, "seq", 1)
    blocks_here = me - side + jnp.arange(2, dtype=jnp.int32)
    ends = jnp.cumsum(item_lengths[0])
    own = jnp.sum((ends[None, :] <= blocks_here[:, None]).astype(jnp.int32), 1)
    labels = jnp.arange(item_lengths.shape[1], dtype=jnp.int32)
    mark = labels[None, :] == own[:, None]
    length = jnp.sum(jnp.where(mark, item_lengths[0][None, :], 0), 1)
    end = jnp.sum(jnp.where(mark, ends[None, :], 0), 1)
    place = jnp.concatenate([blocks_here - (end - length), length, side[None]]).astype(jnp.int32)
    keys = ITEM_MOST * rows
    turns = keys + rows
    shift = jnp.arange(turns, dtype=jnp.int32)
    relative = jnp.where(shift < keys, shift, shift - turns)[None, :] - place[:2, None] * rows
    onehot = (
        bucket_of(relative)[:, :, None] == jnp.arange(BUCKETS, dtype=jnp.int32)[None, None, :]
    ).astype(f32)
    table = jnp.where(
        side == 0,
        rel_table[:, :3],
        jnp.concatenate([rel_table[:, 4:6], rel_table[:, 3:4]], 1),
    )
    by_shift = jnp.sum(onehot[:, None] * table.T[None, :, None, :], -1)
    bias = window_bias(place, by_shift, rows)

    got = after(got, bias)
    keyvals, first, second = paired(side[None], mine, got)
    pieces = [
        passed_along(second, "seq", 4),
        passed_along(keyvals, "seq", 2),
        keyvals,
        passed_along(keyvals, "seq", -2),
        passed_along(first, "seq", -4),
    ]

    attended, attended_other, prob, window = attend(place, mine, got, pieces, bias)
    attended_got = swapped(attended_other, "seq", 1)
    upstream = turned_rows(after(cotangent, attended))
    middle, hidden_two = middle_part(
        side[None], attended, attended_got, inputs, w_out, gain_ffn
    )
    hidden_far = swapped(hidden_two, "seq", pair)
    hidden_got = swapped(hidden_two, "seq", 1)
    hidden_far_got = swapped(hidden_far, "seq", 1)
    upstream_far = swapped(upstream, "seq", third)
    hidden_one_far = swapped(hidden_one, "seq", 1)

    mixed_first, back_first, *sums = ffn_half(
        False, jnp.stack([side, 1 - half]), hidden_two, upstream, w_gateup, w_down
    )
    back_far = swapped(back_first, "seq", pair)
    sums = after(tuple(sums), hidden_far, upstream_far, hidden_got)
    mixed_second, back, output, gain_ffn_grad, middle_back, branch, back_mine, back_other = ffn_half(
        True,
        jnp.stack([side, half]),
        hidden_two,
        upstream,
        w_gateup,
        w_down,
        (*sums, middle, gain_ffn, w_out, cotangent),
    )
    same = half == down_half
    mixed_far = swapped(jnp.where(same, mixed_first, mixed_second), "seq", third)
    back_got = swapped(back_other, "seq", 1)
    branch_far = swapped(after(branch, back_got), "seq", 1)
    back_mine = after(back_mine, hidden_one_far, hidden_far_got)

    backs = attend_back(place, mine, got, window, prob, back_mine, back_got)
    query_back, shift_sums = backs[:2]
    sends = backs[2:]

    def over_dp(kept, sent, dims):
        got = swapped(sent, "dp", 1)
        return tuple(
            value.reshape((2,) * dims + (value.shape[0] >> dims, value.shape[1]))
            for value in (kept, got)
        )

    spot = jnp.stack([core, side])
    units = mixed_first.shape[0]
    owned = units * 4 // blocks
    parts = 2 if owned % 32 == 0 else 1

    def other_owners(value):
        value = value.reshape(2, units // owned // 2, 2, owned, rows)
        return chosen(value, 2, 1 - side).reshape(2, units // 2, rows)

    back_got = swapped(other_owners(back), "seq", 1)
    back_far_sent = other_owners(back_far)
    back_far_got = swapped(back_far_sent, "seq", 1)
    down_kept, down_sent = pair_grad(
        jnp.stack([core, same.astype(jnp.int32)]),
        (2, lambda j: (0, j)),
        units // 2,
        1,
        (after(mixed_second, query_back, back_got, back_far_sent)[None], mixed_first[None]),
        mixed_far[None],
        upstream,
        upstream_far,
    )
    down = Halving(
        over_dp(down_kept, down_sent, len(low) + 1),
        [pair, top] + low[-2::-1],
        [pair] + low[-2::-1] + [top],
    )
    sent = down.step(down_kept)
    near_kept, near_sent, *far_grads = quad_grad(
        spot,
        owned,
        parts,
        (after(back, sent), back_far),
        (back_got, back_far_got),
        (hidden_two, hidden_far, hidden_got, hidden_far_got),
    )
    keyval_back, to_close, to_swap = gathered(
        side[None],
        after(sends[2], near_kept),
        passed_along(sends[3], "seq", 2),
        passed_along(sends[1], "seq", -2),
        passed_along(sends[4], "seq", 4),
        passed_along(sends[0], "seq", -4),
        query_back,
    )
    closed_with = swapped(to_swap, "seq", 1)
    gate_dims = [top] + low[:0:-1]
    gate_order = low[:0:-1] + [top]
    near = Halving(over_dp(near_kept, near_sent, len(low)), gate_dims, gate_order)
    far = None
    if parts == 2:
        far = Halving(over_dp(*far_grads, len(low)), gate_dims, gate_order)
    sent = keyval_back
    sent = near.step(sent)
    head_kept, head_sent = heads_grad(
        jnp.stack([core, side]),
        after(keyval_back, sent),
        query_back,
        (attended, attended_other),
        (hidden_one, hidden_one_far),
        (branch, branch_far),
    )
    others = [top, pair] + low[:0:-1]
    count = len(others)
    each = inner // 2

    def by_owner(value):
        def cut(array, bits):
            array = array.reshape((2,) * count + (-1, array.shape[-1]))
            return array.transpose([bits.index(bit) for bit in others] + [count, count + 1])

        asks = [pair] + low[:0:-1] + [top]
        keyvals = [top] + low[:0:-1] + [pair]
        return jnp.concatenate(
            [
                cut(value[:each], asks),
                cut(value[3 * each :], asks),
                cut(value[each : 3 * each], keyvals),
            ],
            -2,
        )

    head = Halving(
        (by_owner(head_kept), by_owner(swapped(head_sent, "dp", 1))),
        others,
        [pair] + low[1:] + [top],
    )
    sent = head_kept
    sent = far.step(sent) if far else sent
    input_back, gain_attn_grad = closed(
        side[None],
        after(to_close, sent),
        closed_with,
        inputs,
        middle_back,
        w_query,
        w_keyval,
        gain_attn,
    )

    sums = jnp.einsum(
        "pmb,phm->bh", onehot, shift_sums[:, :, 0], precision=lax.Precision.HIGHEST
    )
    nothing = jnp.zeros_like(sums)
    table_local = jnp.where(
        side == 0,
        jnp.concatenate([sums, nothing], 1),
        jnp.concatenate([nothing, sums[:, 2:], sums[:, :2]], 1),
    )
    small = jnp.concatenate(
        [gain_attn_grad.reshape(-1), gain_ffn_grad.reshape(-1), table_local.reshape(-1)]
    )
    taken = small.shape[0]
    small = jnp.pad(small, (0, -taken % 128)).reshape(-1, 128)
    small_got = swapped(small, "dp", 1)
    sent = gain_attn_grad
    small_order = low[::-1] + [pair, top]
    chains = [chain for chain in (near, far, down, head) if chain]
    while any(chain.order for chain in chains) or small_order:
        for chain in chains:
            if chain.order:
                sent = chain.step(sent)
            if small_order and chain in (head, near):
                small = small + after(small_got, sent)
                small_got = swapped(small, "seq", small_order.pop(0))
    small = small + after(small_got, sent)

    turn = [
        (i, (i & ~(top | third)) | (third if i & top else 0) | (top if i & third else 0))
        for i in range(blocks)
    ]
    down_grad = lax.ppermute(down.total(), "seq", turn).astype(f32)[:, :part]
    def exchanged(i, bit):
        return (i & ~(1 | bit)) | (1 if i & bit else 0) | (bit if i & 1 else 0)

    own_rows = inner // blocks
    head_sum = head.total()
    asks = lax.ppermute(
        head_sum[: 2 * own_rows], "seq", [(i, exchanged(i, top)) for i in range(blocks)]
    ).astype(f32)
    query_grad = asks[:own_rows, :part].T
    out_grad = asks[own_rows:, :part]
    keyval_grad = (
        lax.ppermute(
            head_sum[2 * own_rows :], "seq", [(i, exchanged(i, pair)) for i in range(blocks)]
        )
        .astype(f32)[:, :part]
        .T
    )
    gateup_grad = jnp.concatenate([one.total(f32)[:, :part].T for one in (near, far) if one], 1)
    small = small.reshape(-1)
    return (
        output.T[None],
        input_back.T[None],
        small[:width],
        small[width : 2 * width],
        small[2 * width : taken].reshape(BUCKETS, H),
        query_grad,
        keyval_grad,
        out_grad,
        gateup_grad,
        down_grad,
    )


def solution(mesh):
    placed = (
        P("dp", "seq", None),
        P("dp", "seq", None),
        P("dp", None),
        P(),
        P(),
        P(),
        P(),
        P(),
        P(),
        P(),
        P(),
    )
    return jax.shard_map(
        on_device,
        mesh=mesh,
        in_specs=placed,
        out_specs=(
            P("dp", "seq", None),
            P("dp", "seq", None),
            P(),
            P(),
            P(),
            P("dp", "seq"),
            P("dp", "seq"),
            P("seq", "dp"),
            P("dp", "seq"),
            P("seq", "dp"),
        ),
        check_vma=False,
    )
```

profile of v0, /device:TPU:2, one launch (start us, length us, event | category | flops | bytes accessed | tf_op | source)
XLA Modules:
  0.0 289.1 jit_solution(17829000146612629554)
XLA Ops:
  2.0 4.9 %shard_map.186 = (bf16[256,1536]{1,0:T(8,128)(2,1)}, bf16[256,640]{1,0:T(8,128)(2,1)}, bf16[256,640]{1,0:T(8,128)(2,1)}) custom-call(s32[1]{0:T(128)} %bitcast.spot_ref, bf16[1472,256]{1,0:T(8,128)(2,1)} %bitcast.195, f32[1,1472]{1,0:T(1,128)} %broadcast_in_dim.68.gain_ref, bf16[1472,384]{1,0:T(8,128)(2,1)} %w_query_ref.3, bf16[1472,768]{1,0:T(8,128)(2,1)} %w_keyval_ref.3), custom_call_target="tpu_custom_call" | custom-call | flops 24999999488 | tf_op jit(solution)/shard_map/pallas_call | solution.py:161
  9.7 5.9 %shard_map.187.bias_ref = f32[2,3,256,1024]{3,2,1,0:T(8,128)} custom-call(s32[5]{0:T(128)} %pad_add_fusion.1.place_ref, f32[2,3,1,1280]{3,2,1,0:T(1,128)} %copy.47.by_shift_ref), custom_call_target="tpu_custom_call" | custom-call | flops 30000001024 | tf_op jit(solution)/shard_map/pallas_call | solution.py:211
  19.3 3.4 %collective-permute-start.2 = (bf16[512,384]{1,0:T(8,128)(2,1)}, bf16[512,384]{1,0:T(8,128)(2,1)S(1)}, u32[]{:S(2)}, u32[]{:S(2)}) collective-permute-start(bf16[512,384]{1,0:T(8,128)(2,1)} %get-tuple-element.84.pair_ref), channel_id=1, source_target_pairs={{0,4},{2,6},{4,8},{6,10},{8,12},{10,14},{12,16},{14,18},{16,20},{1... | collective-permute-start | bytes 1179656 | tf_op jit(solution)/shard_map/ppermute | solution.py:927
  25.8 5.5 %collective-permute-start.1 = (bf16[256,384]{1,0:T(8,128)(2,1)}, bf16[256,384]{1,0:T(8,128)(2,1)S(1)}, u32[]{:S(2)}, u32[]{:S(2)}) collective-permute-start(bf16[256,384]{1,0:T(8,128)(2,1)} %get-tuple-element.83), channel_id=1, source_target_pairs={{0,8},{2,10},{4,12},{6,14},{8,16},{10,18},{12,20},{14,22},{16,24},... | collective-permute-start | bytes 589832 | tf_op jit(solution)/shard_map/ppermute | solution.py:927
  34.7 5.2 %collective-permute-done.4.ahead_far = bf16[256,384]{1,0:T(8,128)(2,1)S(1)} collective-permute-done((bf16[256,384]{1,0:T(8,128)(2,1)}, bf16[256,384]{1,0:T(8,128)(2,1)S(1)}, u32[]{:S(2)}, u32[]{:S(2)}) %collective-permute-start.4) | collective-permute-done | bytes 196640 | tf_op jit(solution)/shard_map/ppermute | solution.py:927
  41.5 9.8 %shard_map.189 = (bf16[192,256]{1,0:T(8,128)(2,1)}, bf16[192,256]{1,0:T(8,128)(2,1)}, f32[2,3,256,1024]{3,2,1,0:T(8,128)}, bf16[2048,384]{1,0:T(8,128)(2,1)}) custom-call(s32[5]{0:T(128)} %pad_add_fusion.1.place_ref, bf16[256,640]{1,0:T(8,128)(2,1)} %get-tuple-element.80.mine_ref, bf16[256,640]{1,0:T(8,128)(2,1)} %copy-done.26, bf16[256,384]{1,0:T(8,128)(2,1)} %copy-done.32, ...), custom_call_target="tpu_custom_call" | custom-call | flops 44999999488 | tf_op jit(solution)/shard_map/pallas_call | solution.py:323
  52.7 2.3 shard_map.191.upstream_ref.refs_3_
  57.1 3.6 %shard_map.190 = (f32[1472,256]{1,0:T(8,128)}, bf16[256,1536]{1,0:T(8,128)(2,1)}) custom-call(s32[1]{0:T(128)} %bitcast.spot_ref, bf16[192,256]{1,0:T(8,128)(2,1)} %get-tuple-element.86.mine_ref.attended_own, bf16[192,256]{1,0:T(8,128)(2,1)} %copy-done.35, bf16[1472,256]{1,0:T(8,128)(2,1)} %bitcast.196, bf16[1472,384]{1,0:T(8,128)(2,1)} %bitcast.190, ...), custom_call_target="tpu_custom_call" | custom-call | flops 20000000000 | tf_op jit(solution)/shard_map/pallas_call | solution.py:377
  63.7 17.4 %shard_map.192 = (bf16[1792,256]{1,0:T(8,128)(2,1)}, bf16[2,1792,256]{2,1,0:T(8,128)(2,1)}, f32[1472,256]{1,0:T(8,128)}, f32[1472,256]{1,0:T(8,128)}) custom-call(s32[2]{0:T(128)} %get-tuple-element.197.spot_ref, bf16[256,1536]{1,0:T(8,128)(2,1)} %get-tuple-element.88.hidden_ref.refs_0_, bf16[256,1536]{1,0:T(8,128)(2,1)} %shard_map.191.upstream_ref.refs_3_, ...), custom_call_target="tpu_custom_call" | custom-call | flops 99999997952 | tf_op jit(solution)/shard_map/pallas_call | solution.py:522
  82.4 21.8 %shard_map.193 = (bf16[1792,256]{1,0:T(8,128)(2,1)}, bf16[2,1792,256]{2,1,0:T(8,128)(2,1)}, bf16[1472,256]{1,0:T(8,128)(2,1)}, f32[1,1472]{1,0:T(1,128)}, f32[14...) custom-call(s32[2]{0:T(128)} %get-tuple-element.196.spot_ref, ...), custom_call_target="tpu_custom_call" | custom-call | flops 99999997952 | tf_op jit(solution)/shard_map/pallas_call | solution.py:522
  111.5 10.5 %shard_map.194 = (bf16[2,192,256]{2,1,0:T(8,128)(2,1)}, f32[2,3,1,1280]{3,2,1,0:T(1,128)}, bf16[384,256]{1,0:T(8,128)(2,1)}, bf16[384,512]{1,0:T(8,128)(2,1)}, f...) custom-call(s32[5]{0:T(128)} %pad_add_fusion.1.place_ref, ...), custom_call_target="tpu_custom_call" | custom-call | flops 17999998976 | tf_op jit(solution)/shard_map/pallas_call | solution.py:778
  123.1 5.3 %collective-permute-done.12.left_own_got = bf16[2,896,256]{2,1,0:T(8,128)(2,1)S(1)} collective-permute-done((bf16[2,896,256]{2,1,0:T(8,128)(2,1)S(1)}, bf16[2,896,256]{2,1,0:T(8,128)(2,1)S(1)}, u32[]{:S(2)}, u32[]{:S(2)}) %collective-permute-start.12) | collective-permute-done | bytes 917536 | tf_op jit(solution)/shard_map/ppermute | solution.py:921
  129.4 7.2 %shard_map.195 = (bf16[1792,768]{1,0:T(8,128)(2,1)}, bf16[1792,768]{1,0:T(8,128)(2,1)}) custom-call(s32[2]{0:T(128)} %pad_add_fusion.4.spot_ref, bf16[1,1792,256]{2,1,0:T(8,128)(2,1)} %bitcast.178, bf16[1,1792,256]{2,1,0:T(8,128)(2,1)} %bitcast.177, bf16[1,1792,256]{2,1,0:T(8,128)(2,1)} %bitcast.192, bf16[256,1536]{1,0:T(8,128)(2,1)} %shard_map.191.upstream_ref.refs_3_, ...), custom_call_target="tpu_custom_call" | custom-call | flops 120000004096 | tf_op jit(solution)/shard_map/pallas_call | solution.py:579
  140.3 2.9 %collective-permute-start.17 = (bf16[384,512]{1,0:T(8,128)(2,1)S(1)}, bf16[384,512]{1,0:T(8,128)(2,1)}, u32[]{:S(2)}, u32[]{:S(2)}) collective-permute-start(bf16[384,512]{1,0:T(8,128)(2,1)S(1)} %copy-done.23), channel_id=1, source_target_pairs={{0,4},{2,6},{4,8},{6,10},{8,12},{10,14},{12,16},{14,18},{16,20},{1... | collective-permute-start | bytes 1179656 | tf_op jit(solution)/shard_map/ppermute | solution.py:927
  145.4 6.0 %collective-permute-start.19 = (bf16[384,256]{1,0:T(8,128)(2,1)S(1)}, bf16[384,256]{1,0:T(8,128)(2,1)S(1)}, u32[]{:S(2)}, u32[]{:S(2)}) collective-permute-start(bf16[384,256]{1,0:T(8,128)(2,1)S(1)} %copy-done.29), channel_id=1, source_target_pairs={{0,8},{2,10},{4,12},{6,14},{8,16},{10,18},{12,20},{14,22},{16,24},... | collective-permute-start | bytes 589832 | tf_op jit(solution)/shard_map/ppermute | solution.py:927
  151.4 2.8 fusion
  154.2 6.0 %collective-permute-done.16.left_far_got = bf16[2,896,256]{2,1,0:T(8,128)(2,1)} collective-permute-done((bf16[2,896,256]{2,1,0:T(8,128)(2,1)}, bf16[2,896,256]{2,1,0:T(8,128)(2,1)}, u32[]{:S(2)}, u32[]{:S(2)}) %collective-permute-start.16) | collective-permute-done | bytes 917536 | tf_op jit(solution)/shard_map/ppermute | solution.py:921
  161.5 10.8 %shard_map.196 = (bf16[896,768]{1,0:T(8,128)(2,1)}, bf16[896,768]{1,0:T(8,128)(2,1)}, bf16[896,768]{1,0:T(8,128)(2,1)}, bf16[896,768]{1,0:T(8,128)(2,1)}) custom-call(s32[2]{0:T(128)} %pad_add_fusion.3.spot_ref, bf16[2,1792,256]{2,1,0:T(8,128)(2,1)} %get-tuple-element.112.left_own, bf16[2,1792,256]{2,1,0:T(8,128)(2,1)} %copy-done.8, ...), custom_call_target="tpu_custom_call" | custom-call | flops 60000002048 | tf_op jit(solution)/shard_map/pallas_call | solution.py:622
  172.3 2.7 collective-permute-start.29
  175.7 2.9 %shard_map.197 = (bf16[384,512]{1,0:T(8,128)(2,1)}, bf16[576,256]{1,0:T(8,128)(2,1)}, bf16[576,256]{1,0:T(8,128)(2,1)}) custom-call(s32[1]{0:T(128)} %bitcast.spot_ref, f32[384,512]{1,0:T(8,128)} %get-tuple-element.114.pair_ref, bf16[384,512]{1,0:T(8,128)(2,1)} %collective-permute-done.17.behind, bf16[384,512]{1,0:T(8,128)(2,1)} %collective-permute-done.18.ahead, ...), custom_call_target="tpu_custom_call" | custom-call | flops 15000000512 | tf_op jit(solution)/shard_map/pallas_call | solution.py:842
  183.1 6.1 %shard_map.198 = (bf16[768,768]{1,0:T(8,128)(2,1)}, bf16[768,768]{1,0:T(8,128)(2,1)}) custom-call(s32[2]{0:T(128)} %pad_add_fusion.3.spot_ref, bf16[384,512]{1,0:T(8,128)(2,1)} %get-tuple-element.125.keyval_ref, bf16[2,192,256]{2,1,0:T(8,128)(2,1)} %get-tuple-element.105.query_ref, bf16[192,256]{1,0:T(8,128)(2,1)} %get-tuple-element.86.mine_ref.attended_own, ...), custom_call_target="tpu_custom_call" | custom-call | flops 10499999744 | tf_op jit(solution)/shard_map/pallas_call | solution.py:708
  192.2 6.1 %shard_map.199 = (bf16[1472,256]{1,0:T(8,128)(2,1)}, f32[1,1472]{1,0:T(1,128)}) custom-call(s32[1]{0:T(128)} %bitcast.spot_ref, bf16[576,256]{1,0:T(8,128)(2,1)} %get-tuple-element.130.mine_ref, bf16[576,256]{1,0:T(8,128)(2,1)} %copy-done.27, bf16[1472,256]{1,0:T(8,128)(2,1)} %bitcast.197, f32[1472,256]{1,0:T(8,128)} %get-tuple-element.132.middle_back_ref, ...), custom_call_target="tpu_custom_call" | custom-call | flops 89999998976 | tf_op jit(solution)/shard_map/pallas_call | solution.py:898
  202.2 2.8 collective-permute-start.40
  205.0 9.3 %collective-permute-done.30 = bf16[2,224,768]{2,1,0:T(8,128)(2,1)} collective-permute-done((bf16[2,224,768]{2,1,0:T(8,128)(2,1)}, bf16[2,224,768]{2,1,0:T(8,128)(2,1)}, u32[]{:S(2)}, u32[]{:S(2)}) %collective-permute-start.30) | collective-permute-done | bytes 688160 | tf_op jit(solution)/shard_map/ppermute | solution.py:921
  215.5 2.8 collective-permute-start.41
  224.6 11.1 %collective-permute-done.34 = bf16[2,224,768]{2,1,0:T(8,128)(2,1)S(1)} collective-permute-done((bf16[2,224,768]{2,1,0:T(8,128)(2,1)S(1)}, bf16[2,224,768]{2,1,0:T(8,128)(2,1)S(1)}, u32[]{:S(2)}, u32[]{:S(2)}) %collective-permute-start.34) | collective-permute-done | bytes 688160 | tf_op jit(solution)/shard_map/ppermute | solution.py:921
  237.7 13.9 %collective-permute-done.42 = bf16[224,768]{1,0:T(8,128)(2,1)S(1)} collective-permute-done((bf16[224,768]{1,0:T(8,128)(2,1)S(1)}, bf16[224,768]{1,0:T(8,128)(2,1)S(1)}, u32[]{:S(2)}, u32[]{:S(2)}) %collective-permute-start.42) | collective-permute-done | bytes 344096 | tf_op jit(solution)/shard_map/ppermute | solution.py:921
  252.4 2.9 collective-permute-done.33
  262.0 8.3 %collective-permute-done.36 = bf16[2,96,768]{2,1,0:T(8,128)(2,1)S(1)} collective-permute-done((bf16[2,96,768]{2,1,0:T(8,128)(2,1)S(1)}, bf16[2,96,768]{2,1,0:T(8,128)(2,1)S(1)}, u32[]{:S(2)}, u32[]{:S(2)}) %collective-permute-start.36) | collective-permute-done | bytes 294944 | tf_op jit(solution)/shard_map/ppermute | solution.py:921
  271.4 5.0 %collective-permute-done.37 = bf16[96,768]{1,0:T(8,128)(2,1)S(1)} collective-permute-done((bf16[96,768]{1,0:T(8,128)(2,1)S(1)}, bf16[96,768]{1,0:T(8,128)(2,1)S(1)}, u32[]{:S(2)}, u32[]{:S(2)}) %collective-permute-start.37) | collective-permute-done | bytes 147488 | tf_op jit(solution)/shard_map/ppermute | solution.py:921
  276.5 3.4 %collective-permute-start.38 = (bf16[48,768]{1,0:T(8,128)(2,1)S(1)}, bf16[48,768]{1,0:T(8,128)(2,1)S(1)}, u32[]{:S(2)}, u32[]{:S(2)}) collective-permute-start(bf16[48,768]{1,0:T(8,128)(2,1)S(1)} %get-tuple-element.193), channel_id=1, source_target_pairs={{0,0},{2,16},{4,4},{6,20},{8,8},{10,24},{12,12},{14,28},{16,2},{18... | collective-permute-start | bytes 221192 | tf_op jit(solution)/shard_map/ppermute | solution.py:1225
  285.8 2.7 collective-permute-done.39
  (217 shorter events, 76.8 us)
Async XLA Ops:
  19.3 20.6 %collective-permute-start.2 = (bf16[512,384]{1,0:T(8,128)(2,1)}, bf16[512,384]{1,0:T(8,128)(2,1)S(1)}, u32[]{:S(2)}, u32[]{:S(2)}) collective-permute-start(bf16[512,384]{1,0:T(8,128)(2,1)} %get-tuple-element.84.pair_ref), channel_id=1, source_target_pairs={{0,4},{2,6},{4,8},{6,10},{8,12},{10,14},{12,16},{14,18},{16,20},{1... | collective-permute-start | bytes 1179656 | tf_op jit(solution)/shard_map/ppermute | solution.py:927
  22.7 17.2 %collective-permute-start.3 = (bf16[512,384]{1,0:T(8,128)(2,1)}, bf16[512,384]{1,0:T(8,128)(2,1)S(1)}, u32[]{:S(2)}, u32[]{:S(2)}) collective-permute-start(bf16[512,384]{1,0:T(8,128)(2,1)} %get-tuple-element.84.pair_ref), channel_id=1, source_target_pairs={{4,0},{6,2},{8,4},{10,6},{12,8},{14,10},{16,12},{18,14},{20,16},{2... | collective-permute-start | bytes 1179656 | tf_op jit(solution)/shard_map/ppermute | solution.py:927
  24.0 83.7 %collective-permute-start.9 = (bf16[256,1536]{1,0:T(8,128)(2,1)}, bf16[256,1536]{1,0:T(8,128)(2,1)}, u32[]{:S(2)}, u32[]{:S(2)}) collective-permute-start(bf16[256,1536]{1,0:T(8,128)(2,1)} %get-tuple-element.99.hidden_own), channel_id=1, source_target_pairs={{0,2},{2,0},{4,6},{6,4},{8,10},{10,8},{12,14},{14,12},{16,18},{18,... | collective-permute-start | bytes 2359304 | tf_op jit(solution)/shard_map/ppermute | solution.py:921
  55.0 26.2 %collective-permute-start.7 = (bf16[256,1536]{1,0:T(8,128)(2,1)}, bf16[256,1536]{1,0:T(8,128)(2,1)S(1)}, u32[]{:S(2)}, u32[]{:S(2)}) collective-permute-start(bf16[256,1536]{1,0:T(8,128)(2,1)} %shard_map.191.upstream_ref.refs_3_), channel_id=1, source_target_pairs={{0,4},{2,6},{4,0},{6,2},{8,12},{10,14},{12,8},{14,10},{16,20},{18,... | collective-permute-start | bytes 2359304 | tf_op jit(solution)/shard_map/ppermute | solution.py:921
  60.7 20.5 %collective-permute-start.6 = (bf16[256,1536]{1,0:T(8,128)(2,1)}, bf16[256,1536]{1,0:T(8,128)(2,1)S(1)}, u32[]{:S(2)}, u32[]{:S(2)}) collective-permute-start(bf16[256,1536]{1,0:T(8,128)(2,1)} %get-tuple-element.88.hidden_ref.refs_0_), channel_id=1, source_target_pairs={{0,8},{2,10},{4,12},{6,14},{8,0},{10,2},{12,4},{14,6},{16,24},{18,... | collective-permute-start | bytes 2359304 | tf_op jit(solution)/shard_map/ppermute | solution.py:921
  62.3 19.0 %collective-permute-start.8 = (bf16[256,1536]{1,0:T(8,128)(2,1)}, bf16[256,1536]{1,0:T(8,128)(2,1)S(1)}, u32[]{:S(2)}, u32[]{:S(2)}) collective-permute-start(bf16[256,1536]{1,0:T(8,128)(2,1)} %get-tuple-element.88.hidden_ref.refs_0_), channel_id=1, source_target_pairs={{0,2},{2,0},{4,6},{6,4},{8,10},{10,8},{12,14},{14,12},{16,18},{18,... | collective-permute-start | bytes 2359304 | tf_op jit(solution)/shard_map/ppermute | solution.py:921
  81.1 40.9 %collective-permute-start.13 = (bf16[2,1792,256]{2,1,0:T(8,128)(2,1)}, bf16[2,1792,256]{2,1,0:T(8,128)(2,1)S(1)}, u32[]{:S(2)}, u32[]{:S(2)}) collective-permute-start(bf16[2,1792,256]{2,1,0:T(8,128)(2,1)} %get-tuple-element.106), channel_id=1, source_target_pairs={{0,8},{2,10},{4,12},{6,14},{8,0},{10,2},{12,4},{14,6},{16,24},{18,... | collective-permute-start | bytes 5505032 | tf_op jit(solution)/shard_map/ppermute | solution.py:921
  81.3 27.6 %collective-permute-start.10 = (bf16[256,1536]{1,0:T(8,128)(2,1)S(1)}, bf16[256,1536]{1,0:T(8,128)(2,1)}, u32[]{:S(2)}, u32[]{:S(2)}) collective-permute-start(bf16[256,1536]{1,0:T(8,128)(2,1)S(1)} %collective-permute-done.6.refs_1_), channel_id=1, source_target_pairs={{0,2},{2,0},{4,6},{6,4},{8,10},{10,8},{12,14},{14,12},{16,18},{18,... | collective-permute-start | bytes 2359304 | tf_op jit(solution)/shard_map/ppermute | solution.py:921
  106.6 21.9 %collective-permute-start.12 = (bf16[2,896,256]{2,1,0:T(8,128)(2,1)S(1)}, bf16[2,896,256]{2,1,0:T(8,128)(2,1)S(1)}, u32[]{:S(2)}, u32[]{:S(2)}) collective-permute-start(bf16[2,896,256]{2,1,0:T(8,128)(2,1)S(1)} %bitcast.179), channel_id=1, source_target_pairs={{0,2},{2,0},{4,6},{6,4},{8,10},{10,8},{12,14},{14,12},{16,18},{18,... | collective-permute-start | bytes 2752520 | tf_op jit(solution)/shard_map/ppermute | solution.py:921
  107.8 20.6 %collective-permute-start.14 = (bf16[1792,256]{1,0:T(8,128)(2,1)S(1)}, bf16[1792,256]{1,0:T(8,128)(2,1)S(1)}, u32[]{:S(2)}, u32[]{:S(2)}) collective-permute-start(bf16[1792,256]{1,0:T(8,128)(2,1)S(1)} %broadcast_select_fusion), channel_id=1, source_target_pairs={{0,4},{2,6},{4,0},{6,2},{8,12},{10,14},{12,8},{14,10},{16,20},{18,... | collective-permute-start | bytes 2752520 | tf_op jit(solution)/shard_map/ppermute | solution.py:921
  136.7 23.5 %collective-permute-start.16 = (bf16[2,896,256]{2,1,0:T(8,128)(2,1)}, bf16[2,896,256]{2,1,0:T(8,128)(2,1)}, u32[]{:S(2)}, u32[]{:S(2)}) collective-permute-start(bf16[2,896,256]{2,1,0:T(8,128)(2,1)} %bitcast.21), channel_id=1, source_target_pairs={{0,2},{2,0},{4,6},{6,4},{8,10},{10,8},{12,14},{14,12},{16,18},{18,... | collective-permute-start | bytes 2752520 | tf_op jit(solution)/shard_map/ppermute | solution.py:921
  138.7 44.4 %collective-permute-start.23 = (bf16[256,1536]{1,0:T(8,128)(2,1)}, bf16[256,1536]{1,0:T(8,128)(2,1)}, u32[]{:S(2)}, u32[]{:S(2)}) collective-permute-start(bf16[256,1536]{1,0:T(8,128)(2,1)} %get-tuple-element.127.branch_own), channel_id=1, source_target_pairs={{0,2},{2,0},{4,6},{6,4},{8,10},{10,8},{12,14},{14,12},{16,18},{18,... | collective-permute-start | bytes 2359304 | tf_op jit(solution)/shard_map/ppermute | solution.py:921
  140.3 34.7 %collective-permute-start.17 = (bf16[384,512]{1,0:T(8,128)(2,1)S(1)}, bf16[384,512]{1,0:T(8,128)(2,1)}, u32[]{:S(2)}, u32[]{:S(2)}) collective-permute-start(bf16[384,512]{1,0:T(8,128)(2,1)S(1)} %copy-done.23), channel_id=1, source_target_pairs={{0,4},{2,6},{4,8},{6,10},{8,12},{10,14},{12,16},{14,18},{16,20},{1... | collective-permute-start | bytes 1179656 | tf_op jit(solution)/shard_map/ppermute | solution.py:927
  143.2 32.3 %collective-permute-start.18 = (bf16[384,512]{1,0:T(8,128)(2,1)}, bf16[384,512]{1,0:T(8,128)(2,1)}, u32[]{:S(2)}, u32[]{:S(2)}) collective-permute-start(bf16[384,512]{1,0:T(8,128)(2,1)} %get-tuple-element.116), channel_id=1, source_target_pairs={{4,0},{6,2},{8,4},{10,6},{12,8},{14,10},{16,12},{18,14},{20,16},{2... | collective-permute-start | bytes 1179656 | tf_op jit(solution)/shard_map/ppermute | solution.py:927
  145.4 26.9 %collective-permute-start.19 = (bf16[384,256]{1,0:T(8,128)(2,1)S(1)}, bf16[384,256]{1,0:T(8,128)(2,1)S(1)}, u32[]{:S(2)}, u32[]{:S(2)}) collective-permute-start(bf16[384,256]{1,0:T(8,128)(2,1)S(1)} %copy-done.29), channel_id=1, source_target_pairs={{0,8},{2,10},{4,12},{6,14},{8,16},{10,18},{12,20},{14,22},{16,24},... | collective-permute-start | bytes 589832 | tf_op jit(solution)/shard_map/ppermute | solution.py:927
  160.2 14.8 %collective-permute-start.20 = (bf16[384,256]{1,0:T(8,128)(2,1)S(1)}, bf16[384,256]{1,0:T(8,128)(2,1)S(1)}, u32[]{:S(2)}, u32[]{:S(2)}) collective-permute-start(bf16[384,256]{1,0:T(8,128)(2,1)S(1)} %copy-done.28), channel_id=1, source_target_pairs={{8,0},{10,2},{12,4},{14,6},{16,8},{18,10},{20,12},{22,14},{24,16},... | collective-permute-start | bytes 589832 | tf_op jit(solution)/shard_map/ppermute | solution.py:927
  172.3 46.0 %collective-permute-start.29 = (bf16[2,2,224,768]{3,2,1,0:T(8,128)(2,1)}, bf16[2,2,224,768]{3,2,1,0:T(8,128)(2,1)}, u32[]{:S(2)}, u32[]{:S(2)}) collective-permute-start(bf16[2,2,224,768]{3,2,1,0:T(8,128)(2,1)} %fusion), channel_id=1, source_target_pairs={{0,8},{2,10},{4,12},{6,14},{8,0},{10,2},{12,4},{14,6},{16,24},{18,... | collective-permute-start | bytes 4128776 | tf_op jit(solution)/shard_map/ppermute | solution.py:921
  175.0 14.1 %collective-permute-start.21 = (bf16[896,768]{1,0:T(8,128)(2,1)}, bf16[896,768]{1,0:T(8,128)(2,1)S(1)}, u32[]{:S(2)}, u32[]{:S(2)}) collective-permute-start(bf16[896,768]{1,0:T(8,128)(2,1)} %get-tuple-element.121), channel_id=1, source_target_pairs={{0,1},{1,0},{2,3},{3,2},{4,5},{5,4},{6,7},{7,6},{8,9},{9,8},{10,11... | collective-permute-start | bytes 4128776 | tf_op jit(solution)/shard_map/ppermute | solution.py:921
  178.6 12.9 %collective-permute-start.24 = (bf16[576,256]{1,0:T(8,128)(2,1)}, bf16[576,256]{1,0:T(8,128)(2,1)S(1)}, u32[]{:S(2)}, u32[]{:S(2)}) collective-permute-start(bf16[576,256]{1,0:T(8,128)(2,1)} %get-tuple-element.131), channel_id=1, source_target_pairs={{0,2},{2,0},{4,6},{6,4},{8,10},{10,8},{12,14},{14,12},{16,18},{18,... | collective-permute-start | bytes 884744 | tf_op jit(solution)/shard_map/ppermute | solution.py:921
  182.3 18.7 %collective-permute-start.26 = (bf16[2,224,768]{2,1,0:T(8,128)(2,1)}, bf16[2,224,768]{2,1,0:T(8,128)(2,1)}, u32[]{:S(2)}, u32[]{:S(2)}) collective-permute-start(bf16[2,224,768]{2,1,0:T(8,128)(2,1)} %get-tuple-element.179), channel_id=1, source_target_pairs={{0,4},{2,6},{4,0},{6,2},{8,12},{10,14},{12,8},{14,10},{16,20},{18,... | collective-permute-start | bytes 2064392 | tf_op jit(solution)/shard_map/ppermute | solution.py:921
  190.4 23.9 %collective-permute-start.30 = (bf16[2,224,768]{2,1,0:T(8,128)(2,1)}, bf16[2,224,768]{2,1,0:T(8,128)(2,1)}, u32[]{:S(2)}, u32[]{:S(2)}) collective-permute-start(bf16[2,224,768]{2,1,0:T(8,128)(2,1)} %get-tuple-element.177), channel_id=1, source_target_pairs={{0,4},{2,6},{4,0},{6,2},{8,12},{10,14},{12,8},{14,10},{16,20},{18,... | collective-permute-start | bytes 2064392 | tf_op jit(solution)/shard_map/ppermute | solution.py:921
  191.5 30.1 %collective-permute-start.28 = (bf16[768,768]{1,0:T(8,128)(2,1)}, bf16[768,768]{1,0:T(8,128)(2,1)}, u32[]{:S(2)}, u32[]{:S(2)}) collective-permute-start(bf16[768,768]{1,0:T(8,128)(2,1)} %get-tuple-element.139), channel_id=1, source_target_pairs={{0,1},{1,0},{2,3},{3,2},{4,5},{5,4},{6,7},{7,6},{8,9},{9,8},{10,11... | collective-permute-start | bytes 3538952 | tf_op jit(solution)/shard_map/ppermute | solution.py:921
  202.2 54.3 %collective-permute-start.40 = (bf16[224,768]{1,0:T(8,128)(2,1)S(1)}, bf16[224,768]{1,0:T(8,128)(2,1)S(1)}, u32[]{:S(2)}, u32[]{:S(2)}) collective-permute-start(bf16[224,768]{1,0:T(8,128)(2,1)S(1)} %get-tuple-element.183), channel_id=1, source_target_pairs={{0,16},{2,18},{4,20},{6,22},{8,24},{10,26},{12,28},{14,30},{16,0},... | collective-permute-start | bytes 1032200 | tf_op jit(solution)/shard_map/ppermute | solution.py:921
  215.5 20.7 %collective-permute-start.41 = (bf16[224,768]{1,0:T(8,128)(2,1)S(1)}, bf16[224,768]{1,0:T(8,128)(2,1)S(1)}, u32[]{:S(2)}, u32[]{:S(2)}) collective-permute-start(bf16[224,768]{1,0:T(8,128)(2,1)S(1)} %get-tuple-element.185), channel_id=1, source_target_pairs={{0,16},{2,18},{4,20},{6,22},{8,24},{10,26},{12,28},{14,30},{16,0},... | collective-permute-start | bytes 1032200 | tf_op jit(solution)/shard_map/ppermute | solution.py:921
  219.9 15.8 %collective-permute-start.34 = (bf16[2,224,768]{2,1,0:T(8,128)(2,1)S(1)}, bf16[2,224,768]{2,1,0:T(8,128)(2,1)S(1)}, u32[]{:S(2)}, u32[]{:S(2)}) collective-permute-start(bf16[2,224,768]{2,1,0:T(8,128)(2,1)S(1)} %get-tuple-element.175), channel_id=1, source_target_pairs={{0,2},{2,0},{4,6},{6,4},{8,10},{10,8},{12,14},{14,12},{16,18},{18,... | collective-permute-start | bytes 2064392 | tf_op jit(solution)/shard_map/ppermute | solution.py:921
  221.3 14.9 %collective-permute-start.27 = (f32[25,128]{1,0:T(8,128)S(1)}, f32[25,128]{1,0:T(8,128)S(1)}, u32[]{:S(2)}, u32[]{:S(2)}) collective-permute-start(f32[25,128]{1,0:T(8,128)S(1)} %fusion.43), channel_id=1, source_target_pairs={{0,4},{2,6},{4,0},{6,2},{8,12},{10,14},{12,8},{14,10},{16,20},{18,... | collective-permute-start | bytes 38408 | tf_op jit(solution)/shard_map/ppermute | solution.py:921
  224.3 30.9 %collective-permute-start.33 = (bf16[2,2,96,768]{3,2,1,0:T(8,128)(2,1)S(1)}, bf16[2,2,96,768]{3,2,1,0:T(8,128)(2,1)S(1)}, u32[]{:S(2)}, u32[]{:S(2)}) collective-permute-start(bf16[2,2,96,768]{3,2,1,0:T(8,128)(2,1)S(1)} %copy.57), channel_id=1, source_target_pairs={{0,8},{2,10},{4,12},{6,14},{8,0},{10,2},{12,4},{14,6},{16,24},{18,... | collective-permute-start | bytes 1769480 | tf_op jit(solution)/shard_map/ppermute | solution.py:921
  235.8 15.8 %collective-permute-start.42 = (bf16[224,768]{1,0:T(8,128)(2,1)S(1)}, bf16[224,768]{1,0:T(8,128)(2,1)S(1)}, u32[]{:S(2)}, u32[]{:S(2)}) collective-permute-start(bf16[224,768]{1,0:T(8,128)(2,1)S(1)} %fusion.20), channel_id=1, source_target_pairs={{0,16},{2,18},{4,20},{6,22},{8,24},{10,26},{12,28},{14,30},{16,0},... | collective-permute-start | bytes 1032200 | tf_op jit(solution)/shard_map/ppermute | solution.py:921
  236.3 20.3 %collective-permute-start.31 = (f32[25,128]{1,0:T(8,128)S(1)}, f32[25,128]{1,0:T(8,128)S(1)}, u32[]{:S(2)}, u32[]{:S(2)}) collective-permute-start(f32[25,128]{1,0:T(8,128)S(1)} %fusion.48), channel_id=1, source_target_pairs={{0,2},{2,0},{4,6},{6,4},{8,10},{10,8},{12,14},{14,12},{16,18},{18,... | collective-permute-start | bytes 38408 | tf_op jit(solution)/shard_map/ppermute | solution.py:921
  251.7 18.8 %collective-permute-start.43 = (bf16[224,768]{1,0:T(8,128)(2,1)S(1)}, bf16[224,768]{1,0:T(8,128)(2,1)S(1)}, u32[]{:S(2)}, u32[]{:S(2)}) collective-permute-start(bf16[224,768]{1,0:T(8,128)(2,1)S(1)} %fusion.6), channel_id=1, source_target_pairs={{0,0},{2,2},{4,16},{6,18},{8,8},{10,10},{12,24},{14,26},{16,4},{18... | collective-permute-start | bytes 1032200 | tf_op jit(solution)/shard_map/ppermute | solution.py:1219
  255.4 14.8 %collective-permute-start.36 = (bf16[2,96,768]{2,1,0:T(8,128)(2,1)S(1)}, bf16[2,96,768]{2,1,0:T(8,128)(2,1)S(1)}, u32[]{:S(2)}, u32[]{:S(2)}) collective-permute-start(bf16[2,96,768]{2,1,0:T(8,128)(2,1)S(1)} %get-tuple-element.187), channel_id=1, source_target_pairs={{0,4},{2,6},{4,0},{6,2},{8,12},{10,14},{12,8},{14,10},{16,20},{18,... | collective-permute-start | bytes 884744 | tf_op jit(solution)/shard_map/ppermute | solution.py:921
  260.4 10.0 %collective-permute-start.35 = (f32[25,128]{1,0:T(8,128)S(1)}, f32[25,128]{1,0:T(8,128)S(1)}, u32[]{:S(2)}, u32[]{:S(2)}) collective-permute-start(f32[25,128]{1,0:T(8,128)S(1)} %add.318), channel_id=1, source_target_pairs={{0,16},{2,18},{4,20},{6,22},{8,24},{10,26},{12,28},{14,30},{16,0},... | collective-permute-start | bytes 38408 | tf_op jit(solution)/shard_map/ppermute | solution.py:921
  (48 other events, 326.0 us)
where the time goes:
time: 290 us; the launch traced here: 289 us
  Pallas kernels  111 us (38%)
  waiting for transfers between devices  77.2 us (27%)
  starting transfers between devices  62 us (21%)
  other arithmetic  19.7 us (7%)
  local copies, waits for them, and re-layouts  17.6 us (6%)
    ppermute x33, waiting for transfers between devices, swapped(): return lax.ppermute(value, axis, [(i, i ^ bit) for i in range(size)])  67.1 us
    pallas_call x2, Pallas kernels, ffn_half(): pl.pallas_call(functools.partial(ffn_kernel, last), grid_spec=pltpu.Prefe...  39.2 us
    ppermute x33, starting transfers between devices, swapped(): return lax.ppermute(value, axis, [(i, i ^ bit) for i in range(size)])  33.1 us
    ppermute x8, starting transfers between devices, passed_along(): return lax.ppermute(value, axis, pairs)  22.9 us
    pallas_call x1, Pallas kernels, quad_grad(): pl.pallas_call(functools.partial(quad_grad_kernel, parts), grid_spec=pltp...  10.8 us
    pallas_call x1, Pallas kernels, attend_back(): pl.pallas_call(attend_back_kernel, grid_spec=pltpu.PrefetchScalarGridSpec...  10.5 us
    pallas_call x1, Pallas kernels, attend(): pl.pallas_call(attend_kernel, grid_spec=pltpu.PrefetchScalarGridSpec(num_...  9.78 us
    convert_element_type x9, other arithmetic, added(): return (left.astype(f32) + right.astype(f32)).astype(bf16)  9.13 us
  transfers between devices with their start and end apart: 44, of which 16 were waited for; matrix products, arithmetic and copies ran while one was open for 10% of the time, Pallas kernels for 34%

commit v1 on v0

--- a/solution.py
+++ b/solution.py
@@ -1044,7 +1044,7 @@
 
     attended, attended_other, prob, window = attend(place, mine, got, pieces, bias)
     attended_got = swapped(attended_other, "seq", 1)
-    upstream = turned_rows(after(cotangent, attended))
+    upstream = turned_rows(after(cotangent, hidden_one))
     middle, hidden_two = middle_part(
         side[None], attended, attended_got, inputs, w_out, gain_ffn
     )
@@ -1170,7 +1170,7 @@
     head = Halving(
         (by_owner(head_kept), by_owner(swapped(head_sent, "dp", 1))),
         others,
-        [pair] + low[1:] + [top],
+        low[1:] + [pair, top],
     )
     sent = head_kept
     sent = far.step(sent) if far else sent

time: 290 us -> 290 us (level)
  starting transfers between devices: 62 us -> 69.6 us
  waiting for transfers between devices: 77.2 us -> 69.7 us
    ppermute x33, starting transfers between devices: 33.1 us -> 41.9 us  [swapped(): return lax.ppermute(value, axis, [(i, i ^ bit) for i in range(size)])]
    ppermute x33, waiting for transfers between devices: 67.1 us -> 61.2 us  [swapped(): return lax.ppermute(value, axis, [(i, i ^ bit) for i in range(size)])]
    unnamed x73 -> x71, local copies, waits for them, and re-layouts: 7.35 us -> 7.31 us
where the time goes in v1:
time: 290 us; the launch traced here: 289 us
  Pallas kernels  111 us (38%)
  waiting for transfers between devices  69.7 us (24%)
  starting transfers between devices  69.6 us (24%)
  other arithmetic  19.7 us (7%)
  local copies, waits for them, and re-layouts  17.5 us (6%)
    ppermute x33, waiting for transfers between devices, swapped(): return lax.ppermute(value, axis, [(i, i ^ bit) for i in range(size)])  61.2 us
    ppermute x33, starting transfers between devices, swapped(): return lax.ppermute(value, axis, [(i, i ^ bit) for i in range(size)])  41.9 us
    pallas_call x2, Pallas kernels, ffn_half(): pl.pallas_call(functools.partial(ffn_kernel, last), grid_spec=pltpu.Prefe...  39.1 us
    ppermute x8, starting transfers between devices, passed_along(): return lax.ppermute(value, axis, pairs)  23.1 us
    pallas_call x1, Pallas kernels, quad_grad(): pl.pallas_call(functools.partial(quad_grad_kernel, parts), grid_spec=pltp...  10.8 us
    pallas_call x1, Pallas kernels, attend_back(): pl.pallas_call(attend_back_kernel, grid_spec=pltpu.PrefetchScalarGridSpec...  10.5 us
    pallas_call x1, Pallas kernels, attend(): pl.pallas_call(attend_kernel, grid_spec=pltpu.PrefetchScalarGridSpec(num_...  9.75 us
    convert_element_type x9, other arithmetic, added(): return (left.astype(f32) + right.astype(f32)).astype(bf16)  9.15 us
  transfers between devices with their start and end apart: 44, of which 16 were waited for; matrix products, arithmetic and copies ran while one was open for 10% of the time, Pallas kernels for 34%

profile of v1, /device:TPU:2, one launch (start us, length us, event | category | flops | bytes accessed | tf_op | source)
XLA Modules:
  0.0 289.2 jit_solution(17554343547372237211)
XLA Ops:
  2.0 4.9 %shard_map.186 = (bf16[256,1536]{1,0:T(8,128)(2,1)}, bf16[256,640]{1,0:T(8,128)(2,1)}, bf16[256,640]{1,0:T(8,128)(2,1)}) custom-call(s32[1]{0:T(128)} %bitcast.spot_ref, bf16[1472,256]{1,0:T(8,128)(2,1)} %bitcast.195, f32[1,1472]{1,0:T(1,128)} %broadcast_in_dim.68.gain_ref, bf16[1472,384]{1,0:T(8,128)(2,1)} %w_query_ref.3, bf16[1472,768]{1,0:T(8,128)(2,1)} %w_keyval_ref.3), custom_call_target="tpu_custom_call" | custom-call | flops 24999999488 | tf_op jit(solution)/shard_map/pallas_call | solution.py:161
  11.6 5.9 %shard_map.187.bias_ref = f32[2,3,256,1024]{3,2,1,0:T(8,128)} custom-call(s32[5]{0:T(128)} %pad_add_fusion.1.place_ref, f32[2,3,1,1280]{3,2,1,0:T(1,128)} %copy.47.by_shift_ref), custom_call_target="tpu_custom_call" | custom-call | flops 30000001024 | tf_op jit(solution)/shard_map/pallas_call | solution.py:211
  20.4 3.4 %collective-permute-start.2 = (bf16[512,384]{1,0:T(8,128)(2,1)}, bf16[512,384]{1,0:T(8,128)(2,1)S(1)}, u32[]{:S(2)}, u32[]{:S(2)}) collective-permute-start(bf16[512,384]{1,0:T(8,128)(2,1)} %get-tuple-element.84.pair_ref), channel_id=1, source_target_pairs={{0,4},{2,6},{4,8},{6,10},{8,12},{10,14},{12,16},{14,18},{16,20},{1... | collective-permute-start | bytes 1179656 | tf_op jit(solution)/shard_map/ppermute | solution.py:927
  25.2 5.5 %collective-permute-start.1 = (bf16[256,384]{1,0:T(8,128)(2,1)}, bf16[256,384]{1,0:T(8,128)(2,1)S(1)}, u32[]{:S(2)}, u32[]{:S(2)}) collective-permute-start(bf16[256,384]{1,0:T(8,128)(2,1)} %get-tuple-element.83), channel_id=1, source_target_pairs={{0,8},{2,10},{4,12},{6,14},{8,16},{10,18},{12,20},{14,22},{16,24},... | collective-permute-start | bytes 589832 | tf_op jit(solution)/shard_map/ppermute | solution.py:927
  37.6 3.4 %collective-permute-done.4.ahead_far = bf16[256,384]{1,0:T(8,128)(2,1)S(1)} collective-permute-done((bf16[256,384]{1,0:T(8,128)(2,1)}, bf16[256,384]{1,0:T(8,128)(2,1)S(1)}, u32[]{:S(2)}, u32[]{:S(2)}) %collective-permute-start.4) | collective-permute-done | bytes 196640 | tf_op jit(solution)/shard_map/ppermute | solution.py:927
  43.6 9.8 %shard_map.189 = (bf16[192,256]{1,0:T(8,128)(2,1)}, bf16[192,256]{1,0:T(8,128)(2,1)}, f32[2,3,256,1024]{3,2,1,0:T(8,128)}, bf16[2048,384]{1,0:T(8,128)(2,1)}) custom-call(s32[5]{0:T(128)} %pad_add_fusion.1.place_ref, bf16[256,640]{1,0:T(8,128)(2,1)} %get-tuple-element.80.mine_ref, bf16[256,640]{1,0:T(8,128)(2,1)} %copy-done.25, bf16[256,384]{1,0:T(8,128)(2,1)} %copy-done.29, ...), custom_call_target="tpu_custom_call" | custom-call | flops 44999999488 | tf_op jit(solution)/shard_map/pallas_call | solution.py:323
  54.5 3.7 %collective-permute-done.5.other_ref = bf16[192,256]{1,0:T(8,128)(2,1)S(1)} collective-permute-done((bf16[192,256]{1,0:T(8,128)(2,1)}, bf16[192,256]{1,0:T(8,128)(2,1)S(1)}, u32[]{:S(2)}, u32[]{:S(2)}) %collective-permute-start.5) | collective-permute-done | bytes 98336 | tf_op jit(solution)/shard_map/ppermute | solution.py:921
  58.8 3.6 %shard_map.190 = (f32[1472,256]{1,0:T(8,128)}, bf16[256,1536]{1,0:T(8,128)(2,1)}) custom-call(s32[1]{0:T(128)} %bitcast.spot_ref, bf16[192,256]{1,0:T(8,128)(2,1)} %get-tuple-element.86.mine_ref.attended_own, bf16[192,256]{1,0:T(8,128)(2,1)} %copy-done.34, bf16[1472,256]{1,0:T(8,128)(2,1)} %bitcast.196, bf16[1472,384]{1,0:T(8,128)(2,1)} %bitcast.190, ...), custom_call_target="tpu_custom_call" | custom-call | flops 20000000000 | tf_op jit(solution)/shard_map/pallas_call | solution.py:377
  64.5 17.4 %shard_map.192 = (bf16[1792,256]{1,0:T(8,128)(2,1)}, bf16[2,1792,256]{2,1,0:T(8,128)(2,1)}, f32[1472,256]{1,0:T(8,128)}, f32[1472,256]{1,0:T(8,128)}) custom-call(s32[2]{0:T(128)} %get-tuple-element.197.spot_ref, bf16[256,1536]{1,0:T(8,128)(2,1)} %get-tuple-element.88.hidden_ref.refs_0_, bf16[256,1536]{1,0:T(8,128)(2,1)} %shard_map.191.upstream_ref.refs_3_, ...), custom_call_target="tpu_custom_call" | custom-call | flops 99999997952 | tf_op jit(solution)/shard_map/pallas_call | solution.py:522
  84.0 21.7 %shard_map.193 = (bf16[1792,256]{1,0:T(8,128)(2,1)}, bf16[2,1792,256]{2,1,0:T(8,128)(2,1)}, bf16[1472,256]{1,0:T(8,128)(2,1)}, f32[1,1472]{1,0:T(1,128)}, f32[14...) custom-call(s32[2]{0:T(128)} %get-tuple-element.196.spot_ref, ...), custom_call_target="tpu_custom_call" | custom-call | flops 99999997952 | tf_op jit(solution)/shard_map/pallas_call | solution.py:522
  113.1 10.5 %shard_map.194 = (bf16[2,192,256]{2,1,0:T(8,128)(2,1)}, f32[2,3,1,1280]{3,2,1,0:T(1,128)}, bf16[384,256]{1,0:T(8,128)(2,1)}, bf16[384,512]{1,0:T(8,128)(2,1)}, f...) custom-call(s32[5]{0:T(128)} %pad_add_fusion.1.place_ref, ...), custom_call_target="tpu_custom_call" | custom-call | flops 17999998976 | tf_op jit(solution)/shard_map/pallas_call | solution.py:778
  124.6 3.7 %collective-permute-done.12.left_own_got = bf16[2,896,256]{2,1,0:T(8,128)(2,1)S(1)} collective-permute-done((bf16[2,896,256]{2,1,0:T(8,128)(2,1)S(1)}, bf16[2,896,256]{2,1,0:T(8,128)(2,1)S(1)}, u32[]{:S(2)}, u32[]{:S(2)}) %collective-permute-start.12) | collective-permute-done | bytes 917536 | tf_op jit(solution)/shard_map/ppermute | solution.py:921
  129.3 7.2 %shard_map.195 = (bf16[1792,768]{1,0:T(8,128)(2,1)}, bf16[1792,768]{1,0:T(8,128)(2,1)}) custom-call(s32[2]{0:T(128)} %pad_add_fusion.4.spot_ref, bf16[1,1792,256]{2,1,0:T(8,128)(2,1)} %bitcast.178, bf16[1,1792,256]{2,1,0:T(8,128)(2,1)} %bitcast.177, bf16[1,1792,256]{2,1,0:T(8,128)(2,1)} %bitcast.192, bf16[256,1536]{1,0:T(8,128)(2,1)} %shard_map.191.upstream_ref.refs_3_, ...), custom_call_target="tpu_custom_call" | custom-call | flops 120000004096 | tf_op jit(solution)/shard_map/pallas_call | solution.py:579
  140.2 2.8 collective-permute-start.17
  145.2 6.3 %collective-permute-start.19 = (bf16[384,256]{1,0:T(8,128)(2,1)S(1)}, bf16[384,256]{1,0:T(8,128)(2,1)S(1)}, u32[]{:S(2)}, u32[]{:S(2)}) collective-permute-start(bf16[384,256]{1,0:T(8,128)(2,1)S(1)} %copy-done.28), channel_id=1, source_target_pairs={{0,8},{2,10},{4,12},{6,14},{8,16},{10,18},{12,20},{14,22},{16,24},... | collective-permute-start | bytes 589832 | tf_op jit(solution)/shard_map/ppermute | solution.py:927
  151.4 2.8 fusion
  154.3 5.9 %collective-permute-done.16.left_far_got = bf16[2,896,256]{2,1,0:T(8,128)(2,1)} collective-permute-done((bf16[2,896,256]{2,1,0:T(8,128)(2,1)}, bf16[2,896,256]{2,1,0:T(8,128)(2,1)}, u32[]{:S(2)}, u32[]{:S(2)}) %collective-permute-start.16) | collective-permute-done | bytes 917536 | tf_op jit(solution)/shard_map/ppermute | solution.py:921
  161.4 10.8 %shard_map.196 = (bf16[896,768]{1,0:T(8,128)(2,1)}, bf16[896,768]{1,0:T(8,128)(2,1)}, bf16[896,768]{1,0:T(8,128)(2,1)}, bf16[896,768]{1,0:T(8,128)(2,1)}) custom-call(s32[2]{0:T(128)} %pad_add_fusion.3.spot_ref, bf16[2,1792,256]{2,1,0:T(8,128)(2,1)} %get-tuple-element.112.left_own, bf16[2,1792,256]{2,1,0:T(8,128)(2,1)} %copy-done.8, ...), custom_call_target="tpu_custom_call" | custom-call | flops 60000002048 | tf_op jit(solution)/shard_map/pallas_call | solution.py:622
  172.2 2.7 collective-permute-start.29
  175.6 2.9 %shard_map.197 = (bf16[384,512]{1,0:T(8,128)(2,1)}, bf16[576,256]{1,0:T(8,128)(2,1)}, bf16[576,256]{1,0:T(8,128)(2,1)}) custom-call(s32[1]{0:T(128)} %bitcast.spot_ref, f32[384,512]{1,0:T(8,128)} %get-tuple-element.114.pair_ref, bf16[384,512]{1,0:T(8,128)(2,1)} %collective-permute-done.17.behind, bf16[384,512]{1,0:T(8,128)(2,1)} %collective-permute-done.18.ahead, ...), custom_call_target="tpu_custom_call" | custom-call | flops 15000000512 | tf_op jit(solution)/shard_map/pallas_call | solution.py:842
  182.8 6.2 %shard_map.198 = (bf16[768,768]{1,0:T(8,128)(2,1)}, bf16[768,768]{1,0:T(8,128)(2,1)}) custom-call(s32[2]{0:T(128)} %pad_add_fusion.3.spot_ref, bf16[384,512]{1,0:T(8,128)(2,1)} %get-tuple-element.125.keyval_ref, bf16[2,192,256]{2,1,0:T(8,128)(2,1)} %get-tuple-element.105.query_ref, bf16[192,256]{1,0:T(8,128)(2,1)} %get-tuple-element.86.mine_ref.attended_own, ...), custom_call_target="tpu_custom_call" | custom-call | flops 10499999744 | tf_op jit(solution)/shard_map/pallas_call | solution.py:708
  192.8 6.1 %shard_map.199 = (bf16[1472,256]{1,0:T(8,128)(2,1)}, f32[1,1472]{1,0:T(1,128)}) custom-call(s32[1]{0:T(128)} %bitcast.spot_ref, bf16[576,256]{1,0:T(8,128)(2,1)} %get-tuple-element.130.mine_ref, bf16[576,256]{1,0:T(8,128)(2,1)} %copy-done.26, bf16[1472,256]{1,0:T(8,128)(2,1)} %bitcast.197, f32[1472,256]{1,0:T(8,128)} %get-tuple-element.132.middle_back_ref, ...), custom_call_target="tpu_custom_call" | custom-call | flops 89999998976 | tf_op jit(solution)/shard_map/pallas_call | solution.py:898
  202.8 2.8 collective-permute-start.40
  205.5 9.3 %collective-permute-done.30 = bf16[2,224,768]{2,1,0:T(8,128)(2,1)} collective-permute-done((bf16[2,224,768]{2,1,0:T(8,128)(2,1)}, bf16[2,224,768]{2,1,0:T(8,128)(2,1)}, u32[]{:S(2)}, u32[]{:S(2)}) %collective-permute-start.30) | collective-permute-done | bytes 688160 | tf_op jit(solution)/shard_map/ppermute | solution.py:921
  216.1 2.8 collective-permute-start.41
  226.1 10.2 %collective-permute-done.34 = bf16[2,224,768]{2,1,0:T(8,128)(2,1)S(1)} collective-permute-done((bf16[2,224,768]{2,1,0:T(8,128)(2,1)S(1)}, bf16[2,224,768]{2,1,0:T(8,128)(2,1)S(1)}, u32[]{:S(2)}, u32[]{:S(2)}) %collective-permute-start.34) | collective-permute-done | bytes 688160 | tf_op jit(solution)/shard_map/ppermute | solution.py:921
  237.6 14.3 %collective-permute-done.42 = bf16[224,768]{1,0:T(8,128)(2,1)S(1)} collective-permute-done((bf16[224,768]{1,0:T(8,128)(2,1)S(1)}, bf16[224,768]{1,0:T(8,128)(2,1)S(1)}, u32[]{:S(2)}, u32[]{:S(2)}) %collective-permute-start.42) | collective-permute-done | bytes 344096 | tf_op jit(solution)/shard_map/ppermute | solution.py:921
  256.4 6.5 %collective-permute-done.32 = f32[25,128]{1,0:T(8,128)S(1)} collective-permute-done((f32[25,128]{1,0:T(8,128)S(1)}, f32[25,128]{1,0:T(8,128)S(1)}, u32[]{:S(2)}, u32[]{:S(2)}) %collective-permute-start.32) | collective-permute-done | bytes 12832 | tf_op jit(solution)/shard_map/ppermute | solution.py:921
  262.9 7.6 %collective-permute-start.35 = (f32[25,128]{1,0:T(8,128)S(1)}, f32[25,128]{1,0:T(8,128)S(1)}, u32[]{:S(2)}, u32[]{:S(2)}) collective-permute-start(f32[25,128]{1,0:T(8,128)S(1)} %add.318), channel_id=1, source_target_pairs={{0,16},{2,18},{4,20},{6,22},{8,24},{10,26},{12,28},{14,30},{16,0},... | collective-permute-start | bytes 38408 | tf_op jit(solution)/shard_map/ppermute | solution.py:921
  270.7 2.7 collective-permute-done.35
  274.3 3.7 %collective-permute-done.37 = bf16[96,768]{1,0:T(8,128)(2,1)S(1)} collective-permute-done((bf16[96,768]{1,0:T(8,128)(2,1)S(1)}, bf16[96,768]{1,0:T(8,128)(2,1)S(1)}, u32[]{:S(2)}, u32[]{:S(2)}) %collective-permute-start.37) | collective-permute-done | bytes 147488 | tf_op jit(solution)/shard_map/ppermute | solution.py:921
  283.4 2.8 collective-permute-done.38
  (215 shorter events, 78.3 us)
Async XLA Ops:
  6.8 10.8 %collective-permute-start = (bf16[256,640]{1,0:T(8,128)(2,1)}, bf16[256,640]{1,0:T(8,128)(2,1)S(1)}, u32[]{:S(2)}, u32[]{:S(2)}) collective-permute-start(bf16[256,640]{1,0:T(8,128)(2,1)} %get-tuple-element.81), channel_id=1, source_target_pairs={{0,2},{2,0},{4,6},{6,4},{8,10},{10,8},{12,14},{14,12},{16,18},{18,... | collective-permute-start | bytes 983048 | tf_op jit(solution)/shard_map/ppermute | solution.py:921
  6.8 102.4 %collective-permute-start.9 = (bf16[256,1536]{1,0:T(8,128)(2,1)}, bf16[256,1536]{1,0:T(8,128)(2,1)}, u32[]{:S(2)}, u32[]{:S(2)}) collective-permute-start(bf16[256,1536]{1,0:T(8,128)(2,1)} %get-tuple-element.89.hidden_own), channel_id=1, source_target_pairs={{0,2},{2,0},{4,6},{6,4},{8,10},{10,8},{12,14},{14,12},{16,18},{18,... | collective-permute-start | bytes 2359304 | tf_op jit(solution)/shard_map/ppermute | solution.py:921
  20.4 21.7 %collective-permute-start.2 = (bf16[512,384]{1,0:T(8,128)(2,1)}, bf16[512,384]{1,0:T(8,128)(2,1)S(1)}, u32[]{:S(2)}, u32[]{:S(2)}) collective-permute-start(bf16[512,384]{1,0:T(8,128)(2,1)} %get-tuple-element.84.pair_ref), channel_id=1, source_target_pairs={{0,4},{2,6},{4,8},{6,10},{8,12},{10,14},{12,16},{14,18},{16,20},{1... | collective-permute-start | bytes 1179656 | tf_op jit(solution)/shard_map/ppermute | solution.py:927
  23.9 18.3 %collective-permute-start.3 = (bf16[512,384]{1,0:T(8,128)(2,1)}, bf16[512,384]{1,0:T(8,128)(2,1)S(1)}, u32[]{:S(2)}, u32[]{:S(2)}) collective-permute-start(bf16[512,384]{1,0:T(8,128)(2,1)} %get-tuple-element.84.pair_ref), channel_id=1, source_target_pairs={{4,0},{6,2},{8,4},{10,6},{12,8},{14,10},{16,12},{18,14},{20,16},{2... | collective-permute-start | bytes 1179656 | tf_op jit(solution)/shard_map/ppermute | solution.py:927
  35.6 46.9 %collective-permute-start.7 = (bf16[256,1536]{1,0:T(8,128)(2,1)}, bf16[256,1536]{1,0:T(8,128)(2,1)}, u32[]{:S(2)}, u32[]{:S(2)}) collective-permute-start(bf16[256,1536]{1,0:T(8,128)(2,1)} %shard_map.191.upstream_ref.refs_3_), channel_id=1, source_target_pairs={{0,4},{2,6},{4,0},{6,2},{8,12},{10,14},{12,8},{14,10},{16,20},{18,... | collective-permute-start | bytes 2359304 | tf_op jit(solution)/shard_map/ppermute | solution.py:921
  62.4 20.0 %collective-permute-start.6 = (bf16[256,1536]{1,0:T(8,128)(2,1)}, bf16[256,1536]{1,0:T(8,128)(2,1)S(1)}, u32[]{:S(2)}, u32[]{:S(2)}) collective-permute-start(bf16[256,1536]{1,0:T(8,128)(2,1)} %get-tuple-element.88.hidden_ref.refs_0_), channel_id=1, source_target_pairs={{0,8},{2,10},{4,12},{6,14},{8,0},{10,2},{12,4},{14,6},{16,24},{18,... | collective-permute-start | bytes 2359304 | tf_op jit(solution)/shard_map/ppermute | solution.py:921
  64.0 18.4 %collective-permute-start.8 = (bf16[256,1536]{1,0:T(8,128)(2,1)}, bf16[256,1536]{1,0:T(8,128)(2,1)S(1)}, u32[]{:S(2)}, u32[]{:S(2)}) collective-permute-start(bf16[256,1536]{1,0:T(8,128)(2,1)} %get-tuple-element.88.hidden_ref.refs_0_), channel_id=1, source_target_pairs={{0,2},{2,0},{4,6},{6,4},{8,10},{10,8},{12,14},{14,12},{16,18},{18,... | collective-permute-start | bytes 2359304 | tf_op jit(solution)/shard_map/ppermute | solution.py:921
  81.9 41.6 %collective-permute-start.13 = (bf16[2,1792,256]{2,1,0:T(8,128)(2,1)}, bf16[2,1792,256]{2,1,0:T(8,128)(2,1)S(1)}, u32[]{:S(2)}, u32[]{:S(2)}) collective-permute-start(bf16[2,1792,256]{2,1,0:T(8,128)(2,1)} %get-tuple-element.106), channel_id=1, source_target_pairs={{0,8},{2,10},{4,12},{6,14},{8,0},{10,2},{12,4},{14,6},{16,24},{18,... | collective-permute-start | bytes 5505032 | tf_op jit(solution)/shard_map/ppermute | solution.py:921
  82.5 29.2 %collective-permute-start.10 = (bf16[256,1536]{1,0:T(8,128)(2,1)S(1)}, bf16[256,1536]{1,0:T(8,128)(2,1)}, u32[]{:S(2)}, u32[]{:S(2)}) collective-permute-start(bf16[256,1536]{1,0:T(8,128)(2,1)S(1)} %collective-permute-done.6.refs_1_), channel_id=1, source_target_pairs={{0,2},{2,0},{4,6},{6,4},{8,10},{10,8},{12,14},{14,12},{16,18},{18,... | collective-permute-start | bytes 2359304 | tf_op jit(solution)/shard_map/ppermute | solution.py:921
  107.6 20.7 %collective-permute-start.12 = (bf16[2,896,256]{2,1,0:T(8,128)(2,1)S(1)}, bf16[2,896,256]{2,1,0:T(8,128)(2,1)S(1)}, u32[]{:S(2)}, u32[]{:S(2)}) collective-permute-start(bf16[2,896,256]{2,1,0:T(8,128)(2,1)S(1)} %bitcast.179), channel_id=1, source_target_pairs={{0,2},{2,0},{4,6},{6,4},{8,10},{10,8},{12,14},{14,12},{16,18},{18,... | collective-permute-start | bytes 2752520 | tf_op jit(solution)/shard_map/ppermute | solution.py:921
  109.3 19.1 %collective-permute-start.14 = (bf16[1792,256]{1,0:T(8,128)(2,1)S(1)}, bf16[1792,256]{1,0:T(8,128)(2,1)S(1)}, u32[]{:S(2)}, u32[]{:S(2)}) collective-permute-start(bf16[1792,256]{1,0:T(8,128)(2,1)S(1)} %broadcast_select_fusion), channel_id=1, source_target_pairs={{0,4},{2,6},{4,0},{6,2},{8,12},{10,14},{12,8},{14,10},{16,20},{18,... | collective-permute-start | bytes 2752520 | tf_op jit(solution)/shard_map/ppermute | solution.py:921
  136.6 23.5 %collective-permute-start.16 = (bf16[2,896,256]{2,1,0:T(8,128)(2,1)}, bf16[2,896,256]{2,1,0:T(8,128)(2,1)}, u32[]{:S(2)}, u32[]{:S(2)}) collective-permute-start(bf16[2,896,256]{2,1,0:T(8,128)(2,1)} %bitcast.21), channel_id=1, source_target_pairs={{0,2},{2,0},{4,6},{6,4},{8,10},{10,8},{12,14},{14,12},{16,18},{18,... | collective-permute-start | bytes 2752520 | tf_op jit(solution)/shard_map/ppermute | solution.py:921
  139.2 43.6 %collective-permute-start.23 = (bf16[256,1536]{1,0:T(8,128)(2,1)}, bf16[256,1536]{1,0:T(8,128)(2,1)}, u32[]{:S(2)}, u32[]{:S(2)}) collective-permute-start(bf16[256,1536]{1,0:T(8,128)(2,1)} %get-tuple-element.127.branch_own), channel_id=1, source_target_pairs={{0,2},{2,0},{4,6},{6,4},{8,10},{10,8},{12,14},{14,12},{16,18},{18,... | collective-permute-start | bytes 2359304 | tf_op jit(solution)/shard_map/ppermute | solution.py:921
  140.2 34.7 %collective-permute-start.17 = (bf16[384,512]{1,0:T(8,128)(2,1)S(1)}, bf16[384,512]{1,0:T(8,128)(2,1)}, u32[]{:S(2)}, u32[]{:S(2)}) collective-permute-start(bf16[384,512]{1,0:T(8,128)(2,1)S(1)} %copy-done.22), channel_id=1, source_target_pairs={{0,4},{2,6},{4,8},{6,10},{8,12},{10,14},{12,16},{14,18},{16,20},{1... | collective-permute-start | bytes 1179656 | tf_op jit(solution)/shard_map/ppermute | solution.py:927
  143.0 32.4 %collective-permute-start.18 = (bf16[384,512]{1,0:T(8,128)(2,1)}, bf16[384,512]{1,0:T(8,128)(2,1)}, u32[]{:S(2)}, u32[]{:S(2)}) collective-permute-start(bf16[384,512]{1,0:T(8,128)(2,1)} %get-tuple-element.116), channel_id=1, source_target_pairs={{4,0},{6,2},{8,4},{10,6},{12,8},{14,10},{16,12},{18,14},{20,16},{2... | collective-permute-start | bytes 1179656 | tf_op jit(solution)/shard_map/ppermute | solution.py:927
  145.2 27.1 %collective-permute-start.19 = (bf16[384,256]{1,0:T(8,128)(2,1)S(1)}, bf16[384,256]{1,0:T(8,128)(2,1)S(1)}, u32[]{:S(2)}, u32[]{:S(2)}) collective-permute-start(bf16[384,256]{1,0:T(8,128)(2,1)S(1)} %copy-done.28), channel_id=1, source_target_pairs={{0,8},{2,10},{4,12},{6,14},{8,16},{10,18},{12,20},{14,22},{16,24},... | collective-permute-start | bytes 589832 | tf_op jit(solution)/shard_map/ppermute | solution.py:927
  160.1 14.8 %collective-permute-start.20 = (bf16[384,256]{1,0:T(8,128)(2,1)S(1)}, bf16[384,256]{1,0:T(8,128)(2,1)S(1)}, u32[]{:S(2)}, u32[]{:S(2)}) collective-permute-start(bf16[384,256]{1,0:T(8,128)(2,1)S(1)} %copy-done.27), channel_id=1, source_target_pairs={{8,0},{10,2},{12,4},{14,6},{16,8},{18,10},{20,12},{22,14},{24,16},... | collective-permute-start | bytes 589832 | tf_op jit(solution)/shard_map/ppermute | solution.py:927
  172.2 46.6 %collective-permute-start.29 = (bf16[2,2,224,768]{3,2,1,0:T(8,128)(2,1)}, bf16[2,2,224,768]{3,2,1,0:T(8,128)(2,1)}, u32[]{:S(2)}, u32[]{:S(2)}) collective-permute-start(bf16[2,2,224,768]{3,2,1,0:T(8,128)(2,1)} %fusion), channel_id=1, source_target_pairs={{0,8},{2,10},{4,12},{6,14},{8,0},{10,2},{12,4},{14,6},{16,24},{18,... | collective-permute-start | bytes 4128776 | tf_op jit(solution)/shard_map/ppermute | solution.py:921
  175.0 14.1 %collective-permute-start.21 = (bf16[896,768]{1,0:T(8,128)(2,1)}, bf16[896,768]{1,0:T(8,128)(2,1)S(1)}, u32[]{:S(2)}, u32[]{:S(2)}) collective-permute-start(bf16[896,768]{1,0:T(8,128)(2,1)} %get-tuple-element.121), channel_id=1, source_target_pairs={{0,1},{1,0},{2,3},{3,2},{4,5},{5,4},{6,7},{7,6},{8,9},{9,8},{10,11... | collective-permute-start | bytes 4128776 | tf_op jit(solution)/shard_map/ppermute | solution.py:921
  178.6 13.5 %collective-permute-start.24 = (bf16[576,256]{1,0:T(8,128)(2,1)}, bf16[576,256]{1,0:T(8,128)(2,1)S(1)}, u32[]{:S(2)}, u32[]{:S(2)}) collective-permute-start(bf16[576,256]{1,0:T(8,128)(2,1)} %get-tuple-element.131), channel_id=1, source_target_pairs={{0,2},{2,0},{4,6},{6,4},{8,10},{10,8},{12,14},{14,12},{16,18},{18,... | collective-permute-start | bytes 884744 | tf_op jit(solution)/shard_map/ppermute | solution.py:921
  182.8 18.7 %collective-permute-start.26 = (bf16[2,224,768]{2,1,0:T(8,128)(2,1)}, bf16[2,224,768]{2,1,0:T(8,128)(2,1)}, u32[]{:S(2)}, u32[]{:S(2)}) collective-permute-start(bf16[2,224,768]{2,1,0:T(8,128)(2,1)} %get-tuple-element.179), channel_id=1, source_target_pairs={{0,4},{2,6},{4,0},{6,2},{8,12},{10,14},{12,8},{14,10},{16,20},{18,... | collective-permute-start | bytes 2064392 | tf_op jit(solution)/shard_map/ppermute | solution.py:921
  190.2 24.6 %collective-permute-start.30 = (bf16[2,224,768]{2,1,0:T(8,128)(2,1)}, bf16[2,224,768]{2,1,0:T(8,128)(2,1)}, u32[]{:S(2)}, u32[]{:S(2)}) collective-permute-start(bf16[2,224,768]{2,1,0:T(8,128)(2,1)} %get-tuple-element.177), channel_id=1, source_target_pairs={{0,4},{2,6},{4,0},{6,2},{8,12},{10,14},{12,8},{14,10},{16,20},{18,... | collective-permute-start | bytes 2064392 | tf_op jit(solution)/shard_map/ppermute | solution.py:921
  192.1 29.4 %collective-permute-start.28 = (bf16[768,768]{1,0:T(8,128)(2,1)}, bf16[768,768]{1,0:T(8,128)(2,1)}, u32[]{:S(2)}, u32[]{:S(2)}) collective-permute-start(bf16[768,768]{1,0:T(8,128)(2,1)} %get-tuple-element.139), channel_id=1, source_target_pairs={{0,1},{1,0},{2,3},{3,2},{4,5},{5,4},{6,7},{7,6},{8,9},{9,8},{10,11... | collective-permute-start | bytes 3538952 | tf_op jit(solution)/shard_map/ppermute | solution.py:921
  202.8 50.3 %collective-permute-start.40 = (bf16[224,768]{1,0:T(8,128)(2,1)S(1)}, bf16[224,768]{1,0:T(8,128)(2,1)S(1)}, u32[]{:S(2)}, u32[]{:S(2)}) collective-permute-start(bf16[224,768]{1,0:T(8,128)(2,1)S(1)} %get-tuple-element.183), channel_id=1, source_target_pairs={{0,16},{2,18},{4,20},{6,22},{8,24},{10,26},{12,28},{14,30},{16,0},... | collective-permute-start | bytes 1032200 | tf_op jit(solution)/shard_map/ppermute | solution.py:921
  216.1 20.7 %collective-permute-start.41 = (bf16[224,768]{1,0:T(8,128)(2,1)S(1)}, bf16[224,768]{1,0:T(8,128)(2,1)S(1)}, u32[]{:S(2)}, u32[]{:S(2)}) collective-permute-start(bf16[224,768]{1,0:T(8,128)(2,1)S(1)} %get-tuple-element.185), channel_id=1, source_target_pairs={{0,16},{2,18},{4,20},{6,22},{8,24},{10,26},{12,28},{14,30},{16,0},... | collective-permute-start | bytes 1032200 | tf_op jit(solution)/shard_map/ppermute | solution.py:921
  220.5 15.8 %collective-permute-start.34 = (bf16[2,224,768]{2,1,0:T(8,128)(2,1)S(1)}, bf16[2,224,768]{2,1,0:T(8,128)(2,1)S(1)}, u32[]{:S(2)}, u32[]{:S(2)}) collective-permute-start(bf16[2,224,768]{2,1,0:T(8,128)(2,1)S(1)} %get-tuple-element.175), channel_id=1, source_target_pairs={{0,2},{2,0},{4,6},{6,4},{8,10},{10,8},{12,14},{14,12},{16,18},{18,... | collective-permute-start | bytes 2064392 | tf_op jit(solution)/shard_map/ppermute | solution.py:921
  221.3 15.5 %collective-permute-start.27 = (f32[25,128]{1,0:T(8,128)S(1)}, f32[25,128]{1,0:T(8,128)S(1)}, u32[]{:S(2)}, u32[]{:S(2)}) collective-permute-start(f32[25,128]{1,0:T(8,128)S(1)} %fusion.43), channel_id=1, source_target_pairs={{0,4},{2,6},{4,0},{6,2},{8,12},{10,14},{12,8},{14,10},{16,20},{18,... | collective-permute-start | bytes 38408 | tf_op jit(solution)/shard_map/ppermute | solution.py:921
  224.3 28.5 %collective-permute-start.33 = (bf16[2,2,96,768]{3,2,1,0:T(8,128)(2,1)S(1)}, bf16[2,2,96,768]{3,2,1,0:T(8,128)(2,1)S(1)}, u32[]{:S(2)}, u32[]{:S(2)}) collective-permute-start(bf16[2,2,96,768]{3,2,1,0:T(8,128)(2,1)S(1)} %copy.57), channel_id=1, source_target_pairs={{0,4},{2,6},{4,0},{6,2},{8,12},{10,14},{12,8},{14,10},{16,20},{18,... | collective-permute-start | bytes 1769480 | tf_op jit(solution)/shard_map/ppermute | solution.py:921
  236.4 15.6 %collective-permute-start.42 = (bf16[224,768]{1,0:T(8,128)(2,1)S(1)}, bf16[224,768]{1,0:T(8,128)(2,1)S(1)}, u32[]{:S(2)}, u32[]{:S(2)}) collective-permute-start(bf16[224,768]{1,0:T(8,128)(2,1)S(1)} %fusion.20), channel_id=1, source_target_pairs={{0,16},{2,18},{4,20},{6,22},{8,24},{10,26},{12,28},{14,30},{16,0},... | collective-permute-start | bytes 1032200 | tf_op jit(solution)/shard_map/ppermute | solution.py:921
  236.8 16.3 %collective-permute-start.31 = (f32[25,128]{1,0:T(8,128)S(1)}, f32[25,128]{1,0:T(8,128)S(1)}, u32[]{:S(2)}, u32[]{:S(2)}) collective-permute-start(f32[25,128]{1,0:T(8,128)S(1)} %fusion.48), channel_id=1, source_target_pairs={{0,2},{2,0},{4,6},{6,4},{8,10},{10,8},{12,14},{14,12},{16,18},{18,... | collective-permute-start | bytes 38408 | tf_op jit(solution)/shard_map/ppermute | solution.py:921
  252.1 21.3 %collective-permute-start.43 = (bf16[224,768]{1,0:T(8,128)(2,1)S(1)}, bf16[224,768]{1,0:T(8,128)(2,1)S(1)}, u32[]{:S(2)}, u32[]{:S(2)}) collective-permute-start(bf16[224,768]{1,0:T(8,128)(2,1)S(1)} %fusion.6), channel_id=1, source_target_pairs={{0,0},{2,2},{4,16},{6,18},{8,8},{10,10},{12,24},{14,26},{16,4},{18... | collective-permute-start | bytes 1032200 | tf_op jit(solution)/shard_map/ppermute | solution.py:1219
  253.0 17.5 %collective-permute-start.36 = (bf16[2,96,768]{2,1,0:T(8,128)(2,1)S(1)}, bf16[2,96,768]{2,1,0:T(8,128)(2,1)S(1)}, u32[]{:S(2)}, u32[]{:S(2)}) collective-permute-start(bf16[2,96,768]{2,1,0:T(8,128)(2,1)S(1)} %get-tuple-element.187), channel_id=1, source_target_pairs={{0,8},{2,10},{4,12},{6,14},{8,0},{10,2},{12,4},{14,6},{16,24},{18,... | collective-permute-start | bytes 884744 | tf_op jit(solution)/shard_map/ppermute | solution.py:921
  (47 other events, 316.1 us)

commit v2 on v1

--- a/solution.py
+++ b/solution.py
@@ -1044,7 +1044,7 @@
 
     attended, attended_other, prob, window = attend(place, mine, got, pieces, bias)
     attended_got = swapped(attended_other, "seq", 1)
-    upstream = turned_rows(after(cotangent, hidden_one))
+    upstream = turned_rows(after(cotangent, attended))
     middle, hidden_two = middle_part(
         side[None], attended, attended_got, inputs, w_out, gain_ffn
     )

time: 290 us -> 290 us (level)
    unnamed x71 -> x73, local copies, waits for them, and re-layouts: 7.31 us -> 7.35 us
  transfers between devices with their start and end apart: 44 -> 44, of which waited for: 16 -> 15; matrix products, arithmetic and copies ran while one was open for 10% -> 10% of each run, Pallas kernels for 34% -> 34%
where the time goes in v2:
time: 290 us; the launch traced here: 289 us
  Pallas kernels  111 us (38%)
  waiting for transfers between devices  70.1 us (24%)
  starting transfers between devices  68.6 us (24%)
  other arithmetic  19.7 us (7%)
  local copies, waits for them, and re-layouts  17.6 us (6%)
    ppermute x33, waiting for transfers between devices, swapped(): return lax.ppermute(value, axis, [(i, i ^ bit) for i in range(size)])  60 us
    ppermute x33, starting transfers between devices, swapped(): return lax.ppermute(value, axis, [(i, i ^ bit) for i in range(size)])  40.8 us
    pallas_call x2, Pallas kernels, ffn_half(): pl.pallas_call(functools.partial(ffn_kernel, last), grid_spec=pltpu.Prefe...  39.2 us
    ppermute x8, starting transfers between devices, passed_along(): return lax.ppermute(value, axis, pairs)  22.9 us
    pallas_call x1, Pallas kernels, quad_grad(): pl.pallas_call(functools.partial(quad_grad_kernel, parts), grid_spec=pltp...  10.8 us
    pallas_call x1, Pallas kernels, attend_back(): pl.pallas_call(attend_back_kernel, grid_spec=pltpu.PrefetchScalarGridSpec...  10.5 us
    pallas_call x1, Pallas kernels, attend(): pl.pallas_call(attend_kernel, grid_spec=pltpu.PrefetchScalarGridSpec(num_...  9.78 us
    convert_element_type x9, other arithmetic, added(): return (left.astype(f32) + right.astype(f32)).astype(bf16)  9.14 us
  transfers between devices with their start and end apart: 44, of which 15 were waited for; matrix products, arithmetic and copies ran while one was open for 10% of the time, Pallas kernels for 34%

profile of v2, /device:TPU:2, one launch (start us, length us, event | category | flops | bytes accessed | tf_op | source)
XLA Modules:
  0.0 288.7 jit_solution(12650128274621354731)
XLA Ops:
  2.0 4.9 %shard_map.186 = (bf16[256,1536]{1,0:T(8,128)(2,1)}, bf16[256,640]{1,0:T(8,128)(2,1)}, bf16[256,640]{1,0:T(8,128)(2,1)}) custom-call(s32[1]{0:T(128)} %bitcast.spot_ref, bf16[1472,256]{1,0:T(8,128)(2,1)} %bitcast.195, f32[1,1472]{1,0:T(1,128)} %broadcast_in_dim.68.gain_ref, bf16[1472,384]{1,0:T(8,128)(2,1)} %w_query_ref.3, bf16[1472,768]{1,0:T(8,128)(2,1)} %w_keyval_ref.3), custom_call_target="tpu_custom_call" | custom-call | flops 24999999488 | tf_op jit(solution)/shard_map/pallas_call | solution.py:161
  9.7 5.9 %shard_map.187.bias_ref = f32[2,3,256,1024]{3,2,1,0:T(8,128)} custom-call(s32[5]{0:T(128)} %pad_add_fusion.1.place_ref, f32[2,3,1,1280]{3,2,1,0:T(1,128)} %copy.47.by_shift_ref), custom_call_target="tpu_custom_call" | custom-call | flops 30000001024 | tf_op jit(solution)/shard_map/pallas_call | solution.py:211
  19.3 3.4 %collective-permute-start.2 = (bf16[512,384]{1,0:T(8,128)(2,1)}, bf16[512,384]{1,0:T(8,128)(2,1)S(1)}, u32[]{:S(2)}, u32[]{:S(2)}) collective-permute-start(bf16[512,384]{1,0:T(8,128)(2,1)} %get-tuple-element.84.pair_ref), channel_id=1, source_target_pairs={{0,4},{2,6},{4,8},{6,10},{8,12},{10,14},{12,16},{14,18},{16,20},{1... | collective-permute-start | bytes 1179656 | tf_op jit(solution)/shard_map/ppermute | solution.py:927
  25.8 5.5 %collective-permute-start.1 = (bf16[256,384]{1,0:T(8,128)(2,1)}, bf16[256,384]{1,0:T(8,128)(2,1)S(1)}, u32[]{:S(2)}, u32[]{:S(2)}) collective-permute-start(bf16[256,384]{1,0:T(8,128)(2,1)} %get-tuple-element.83), channel_id=1, source_target_pairs={{0,8},{2,10},{4,12},{6,14},{8,16},{10,18},{12,20},{14,22},{16,24},... | collective-permute-start | bytes 589832 | tf_op jit(solution)/shard_map/ppermute | solution.py:927
  34.7 5.2 %collective-permute-done.4.ahead_far = bf16[256,384]{1,0:T(8,128)(2,1)S(1)} collective-permute-done((bf16[256,384]{1,0:T(8,128)(2,1)}, bf16[256,384]{1,0:T(8,128)(2,1)S(1)}, u32[]{:S(2)}, u32[]{:S(2)}) %collective-permute-start.4) | collective-permute-done | bytes 196640 | tf_op jit(solution)/shard_map/ppermute | solution.py:927
  41.5 9.8 %shard_map.189 = (bf16[192,256]{1,0:T(8,128)(2,1)}, bf16[192,256]{1,0:T(8,128)(2,1)}, f32[2,3,256,1024]{3,2,1,0:T(8,128)}, bf16[2048,384]{1,0:T(8,128)(2,1)}) custom-call(s32[5]{0:T(128)} %pad_add_fusion.1.place_ref, bf16[256,640]{1,0:T(8,128)(2,1)} %get-tuple-element.80.mine_ref, bf16[256,640]{1,0:T(8,128)(2,1)} %copy-done.26, bf16[256,384]{1,0:T(8,128)(2,1)} %copy-done.32, ...), custom_call_target="tpu_custom_call" | custom-call | flops 44999999488 | tf_op jit(solution)/shard_map/pallas_call | solution.py:323
  52.7 2.3 shard_map.191.upstream_ref.refs_3_
  57.1 3.6 %shard_map.190 = (f32[1472,256]{1,0:T(8,128)}, bf16[256,1536]{1,0:T(8,128)(2,1)}) custom-call(s32[1]{0:T(128)} %bitcast.spot_ref, bf16[192,256]{1,0:T(8,128)(2,1)} %get-tuple-element.86.mine_ref.attended_own, bf16[192,256]{1,0:T(8,128)(2,1)} %copy-done.35, bf16[1472,256]{1,0:T(8,128)(2,1)} %bitcast.196, bf16[1472,384]{1,0:T(8,128)(2,1)} %bitcast.190, ...), custom_call_target="tpu_custom_call" | custom-call | flops 20000000000 | tf_op jit(solution)/shard_map/pallas_call | solution.py:377
  63.7 17.4 %shard_map.192 = (bf16[1792,256]{1,0:T(8,128)(2,1)}, bf16[2,1792,256]{2,1,0:T(8,128)(2,1)}, f32[1472,256]{1,0:T(8,128)}, f32[1472,256]{1,0:T(8,128)}) custom-call(s32[2]{0:T(128)} %get-tuple-element.197.spot_ref, bf16[256,1536]{1,0:T(8,128)(2,1)} %get-tuple-element.88.hidden_ref.refs_0_, bf16[256,1536]{1,0:T(8,128)(2,1)} %shard_map.191.upstream_ref.refs_3_, ...), custom_call_target="tpu_custom_call" | custom-call | flops 99999997952 | tf_op jit(solution)/shard_map/pallas_call | solution.py:522
  82.4 21.8 %shard_map.193 = (bf16[1792,256]{1,0:T(8,128)(2,1)}, bf16[2,1792,256]{2,1,0:T(8,128)(2,1)}, bf16[1472,256]{1,0:T(8,128)(2,1)}, f32[1,1472]{1,0:T(1,128)}, f32[14...) custom-call(s32[2]{0:T(128)} %get-tuple-element.196.spot_ref, ...), custom_call_target="tpu_custom_call" | custom-call | flops 99999997952 | tf_op jit(solution)/shard_map/pallas_call | solution.py:522
  111.5 10.5 %shard_map.194 = (bf16[2,192,256]{2,1,0:T(8,128)(2,1)}, f32[2,3,1,1280]{3,2,1,0:T(1,128)}, bf16[384,256]{1,0:T(8,128)(2,1)}, bf16[384,512]{1,0:T(8,128)(2,1)}, f...) custom-call(s32[5]{0:T(128)} %pad_add_fusion.1.place_ref, ...), custom_call_target="tpu_custom_call" | custom-call | flops 17999998976 | tf_op jit(solution)/shard_map/pallas_call | solution.py:778
  123.1 5.3 %collective-permute-done.12.left_own_got = bf16[2,896,256]{2,1,0:T(8,128)(2,1)S(1)} collective-permute-done((bf16[2,896,256]{2,1,0:T(8,128)(2,1)S(1)}, bf16[2,896,256]{2,1,0:T(8,128)(2,1)S(1)}, u32[]{:S(2)}, u32[]{:S(2)}) %collective-permute-start.12) | collective-permute-done | bytes 917536 | tf_op jit(solution)/shard_map/ppermute | solution.py:921
  129.4 7.2 %shard_map.195 = (bf16[1792,768]{1,0:T(8,128)(2,1)}, bf16[1792,768]{1,0:T(8,128)(2,1)}) custom-call(s32[2]{0:T(128)} %pad_add_fusion.4.spot_ref, bf16[1,1792,256]{2,1,0:T(8,128)(2,1)} %bitcast.178, bf16[1,1792,256]{2,1,0:T(8,128)(2,1)} %bitcast.177, bf16[1,1792,256]{2,1,0:T(8,128)(2,1)} %bitcast.192, bf16[256,1536]{1,0:T(8,128)(2,1)} %shard_map.191.upstream_ref.refs_3_, ...), custom_call_target="tpu_custom_call" | custom-call | flops 120000004096 | tf_op jit(solution)/shard_map/pallas_call | solution.py:579
  140.3 2.9 %collective-permute-start.17 = (bf16[384,512]{1,0:T(8,128)(2,1)S(1)}, bf16[384,512]{1,0:T(8,128)(2,1)}, u32[]{:S(2)}, u32[]{:S(2)}) collective-permute-start(bf16[384,512]{1,0:T(8,128)(2,1)S(1)} %copy-done.23), channel_id=1, source_target_pairs={{0,4},{2,6},{4,8},{6,10},{8,12},{10,14},{12,16},{14,18},{16,20},{1... | collective-permute-start | bytes 1179656 | tf_op jit(solution)/shard_map/ppermute | solution.py:927
  145.4 6.0 %collective-permute-start.19 = (bf16[384,256]{1,0:T(8,128)(2,1)S(1)}, bf16[384,256]{1,0:T(8,128)(2,1)S(1)}, u32[]{:S(2)}, u32[]{:S(2)}) collective-permute-start(bf16[384,256]{1,0:T(8,128)(2,1)S(1)} %copy-done.29), channel_id=1, source_target_pairs={{0,8},{2,10},{4,12},{6,14},{8,16},{10,18},{12,20},{14,22},{16,24},... | collective-permute-start | bytes 589832 | tf_op jit(solution)/shard_map/ppermute | solution.py:927
  151.4 2.8 fusion
  154.2 6.0 %collective-permute-done.16.left_far_got = bf16[2,896,256]{2,1,0:T(8,128)(2,1)} collective-permute-done((bf16[2,896,256]{2,1,0:T(8,128)(2,1)}, bf16[2,896,256]{2,1,0:T(8,128)(2,1)}, u32[]{:S(2)}, u32[]{:S(2)}) %collective-permute-start.16) | collective-permute-done | bytes 917536 | tf_op jit(solution)/shard_map/ppermute | solution.py:921
  161.5 10.8 %shard_map.196 = (bf16[896,768]{1,0:T(8,128)(2,1)}, bf16[896,768]{1,0:T(8,128)(2,1)}, bf16[896,768]{1,0:T(8,128)(2,1)}, bf16[896,768]{1,0:T(8,128)(2,1)}) custom-call(s32[2]{0:T(128)} %pad_add_fusion.3.spot_ref, bf16[2,1792,256]{2,1,0:T(8,128)(2,1)} %get-tuple-element.112.left_own, bf16[2,1792,256]{2,1,0:T(8,128)(2,1)} %copy-done.8, ...), custom_call_target="tpu_custom_call" | custom-call | flops 60000002048 | tf_op jit(solution)/shard_map/pallas_call | solution.py:622
  172.3 2.7 collective-permute-start.29
  175.7 2.9 %shard_map.197 = (bf16[384,512]{1,0:T(8,128)(2,1)}, bf16[576,256]{1,0:T(8,128)(2,1)}, bf16[576,256]{1,0:T(8,128)(2,1)}) custom-call(s32[1]{0:T(128)} %bitcast.spot_ref, f32[384,512]{1,0:T(8,128)} %get-tuple-element.114.pair_ref, bf16[384,512]{1,0:T(8,128)(2,1)} %collective-permute-done.17.behind, bf16[384,512]{1,0:T(8,128)(2,1)} %collective-permute-done.18.ahead, ...), custom_call_target="tpu_custom_call" | custom-call | flops 15000000512 | tf_op jit(solution)/shard_map/pallas_call | solution.py:842
  183.1 6.1 %shard_map.198 = (bf16[768,768]{1,0:T(8,128)(2,1)}, bf16[768,768]{1,0:T(8,128)(2,1)}) custom-call(s32[2]{0:T(128)} %pad_add_fusion.3.spot_ref, bf16[384,512]{1,0:T(8,128)(2,1)} %get-tuple-element.125.keyval_ref, bf16[2,192,256]{2,1,0:T(8,128)(2,1)} %get-tuple-element.105.query_ref, bf16[192,256]{1,0:T(8,128)(2,1)} %get-tuple-element.86.mine_ref.attended_own, ...), custom_call_target="tpu_custom_call" | custom-call | flops 10499999744 | tf_op jit(solution)/shard_map/pallas_call | solution.py:708
  192.2 6.1 %shard_map.199 = (bf16[1472,256]{1,0:T(8,128)(2,1)}, f32[1,1472]{1,0:T(1,128)}) custom-call(s32[1]{0:T(128)} %bitcast.spot_ref, bf16[576,256]{1,0:T(8,128)(2,1)} %get-tuple-element.130.mine_ref, bf16[576,256]{1,0:T(8,128)(2,1)} %copy-done.27, bf16[1472,256]{1,0:T(8,128)(2,1)} %bitcast.197, f32[1472,256]{1,0:T(8,128)} %get-tuple-element.132.middle_back_ref, ...), custom_call_target="tpu_custom_call" | custom-call | flops 89999998976 | tf_op jit(solution)/shard_map/pallas_call | solution.py:898
  202.2 2.8 collective-permute-start.40
  205.0 9.3 %collective-permute-done.30 = bf16[2,224,768]{2,1,0:T(8,128)(2,1)} collective-permute-done((bf16[2,224,768]{2,1,0:T(8,128)(2,1)}, bf16[2,224,768]{2,1,0:T(8,128)(2,1)}, u32[]{:S(2)}, u32[]{:S(2)}) %collective-permute-start.30) | collective-permute-done | bytes 688160 | tf_op jit(solution)/shard_map/ppermute | solution.py:921
  215.5 2.8 collective-permute-start.41
  226.1 9.6 %collective-permute-done.34 = bf16[2,224,768]{2,1,0:T(8,128)(2,1)S(1)} collective-permute-done((bf16[2,224,768]{2,1,0:T(8,128)(2,1)S(1)}, bf16[2,224,768]{2,1,0:T(8,128)(2,1)S(1)}, u32[]{:S(2)}, u32[]{:S(2)}) %collective-permute-start.34) | collective-permute-done | bytes 688160 | tf_op jit(solution)/shard_map/ppermute | solution.py:921
  237.7 13.6 %collective-permute-done.42 = bf16[224,768]{1,0:T(8,128)(2,1)S(1)} collective-permute-done((bf16[224,768]{1,0:T(8,128)(2,1)S(1)}, bf16[224,768]{1,0:T(8,128)(2,1)S(1)}, u32[]{:S(2)}, u32[]{:S(2)}) %collective-permute-start.42) | collective-permute-done | bytes 344096 | tf_op jit(solution)/shard_map/ppermute | solution.py:921
  255.7 6.6 %collective-permute-done.32 = f32[25,128]{1,0:T(8,128)S(1)} collective-permute-done((f32[25,128]{1,0:T(8,128)S(1)}, f32[25,128]{1,0:T(8,128)S(1)}, u32[]{:S(2)}, u32[]{:S(2)}) %collective-permute-start.32) | collective-permute-done | bytes 12832 | tf_op jit(solution)/shard_map/ppermute | solution.py:921
  262.3 7.5 %collective-permute-start.35 = (f32[25,128]{1,0:T(8,128)S(1)}, f32[25,128]{1,0:T(8,128)S(1)}, u32[]{:S(2)}, u32[]{:S(2)}) collective-permute-start(f32[25,128]{1,0:T(8,128)S(1)} %add.318), channel_id=1, source_target_pairs={{0,16},{2,18},{4,20},{6,22},{8,24},{10,26},{12,28},{14,30},{16,0},... | collective-permute-start | bytes 38408 | tf_op jit(solution)/shard_map/ppermute | solution.py:921
  269.9 2.7 collective-permute-done.35
  273.5 3.7 %collective-permute-done.37 = bf16[96,768]{1,0:T(8,128)(2,1)S(1)} collective-permute-done((bf16[96,768]{1,0:T(8,128)(2,1)S(1)}, bf16[96,768]{1,0:T(8,128)(2,1)S(1)}, u32[]{:S(2)}, u32[]{:S(2)}) %collective-permute-start.37) | collective-permute-done | bytes 147488 | tf_op jit(solution)/shard_map/ppermute | solution.py:921
  282.8 2.5 collective-permute-done.38
  (217 shorter events, 77.4 us)
Async XLA Ops:
  19.3 20.6 %collective-permute-start.2 = (bf16[512,384]{1,0:T(8,128)(2,1)}, bf16[512,384]{1,0:T(8,128)(2,1)S(1)}, u32[]{:S(2)}, u32[]{:S(2)}) collective-permute-start(bf16[512,384]{1,0:T(8,128)(2,1)} %get-tuple-element.84.pair_ref), channel_id=1, source_target_pairs={{0,4},{2,6},{4,8},{6,10},{8,12},{10,14},{12,16},{14,18},{16,20},{1... | collective-permute-start | bytes 1179656 | tf_op jit(solution)/shard_map/ppermute | solution.py:927
  22.7 17.2 %collective-permute-start.3 = (bf16[512,384]{1,0:T(8,128)(2,1)}, bf16[512,384]{1,0:T(8,128)(2,1)S(1)}, u32[]{:S(2)}, u32[]{:S(2)}) collective-permute-start(bf16[512,384]{1,0:T(8,128)(2,1)} %get-tuple-element.84.pair_ref), channel_id=1, source_target_pairs={{4,0},{6,2},{8,4},{10,6},{12,8},{14,10},{16,12},{18,14},{20,16},{2... | collective-permute-start | bytes 1179656 | tf_op jit(solution)/shard_map/ppermute | solution.py:927
  24.0 83.7 %collective-permute-start.9 = (bf16[256,1536]{1,0:T(8,128)(2,1)}, bf16[256,1536]{1,0:T(8,128)(2,1)}, u32[]{:S(2)}, u32[]{:S(2)}) collective-permute-start(bf16[256,1536]{1,0:T(8,128)(2,1)} %get-tuple-element.99.hidden_own), channel_id=1, source_target_pairs={{0,2},{2,0},{4,6},{6,4},{8,10},{10,8},{12,14},{14,12},{16,18},{18,... | collective-permute-start | bytes 2359304 | tf_op jit(solution)/shard_map/ppermute | solution.py:921
  55.0 26.2 %collective-permute-start.7 = (bf16[256,1536]{1,0:T(8,128)(2,1)}, bf16[256,1536]{1,0:T(8,128)(2,1)S(1)}, u32[]{:S(2)}, u32[]{:S(2)}) collective-permute-start(bf16[256,1536]{1,0:T(8,128)(2,1)} %shard_map.191.upstream_ref.refs_3_), channel_id=1, source_target_pairs={{0,4},{2,6},{4,0},{6,2},{8,12},{10,14},{12,8},{14,10},{16,20},{18,... | collective-permute-start | bytes 2359304 | tf_op jit(solution)/shard_map/ppermute | solution.py:921
  60.7 20.5 %collective-permute-start.6 = (bf16[256,1536]{1,0:T(8,128)(2,1)}, bf16[256,1536]{1,0:T(8,128)(2,1)S(1)}, u32[]{:S(2)}, u32[]{:S(2)}) collective-permute-start(bf16[256,1536]{1,0:T(8,128)(2,1)} %get-tuple-element.88.hidden_ref.refs_0_), channel_id=1, source_target_pairs={{0,8},{2,10},{4,12},{6,14},{8,0},{10,2},{12,4},{14,6},{16,24},{18,... | collective-permute-start | bytes 2359304 | tf_op jit(solution)/shard_map/ppermute | solution.py:921
  62.3 19.0 %collective-permute-start.8 = (bf16[256,1536]{1,0:T(8,128)(2,1)}, bf16[256,1536]{1,0:T(8,128)(2,1)S(1)}, u32[]{:S(2)}, u32[]{:S(2)}) collective-permute-start(bf16[256,1536]{1,0:T(8,128)(2,1)} %get-tuple-element.88.hidden_ref.refs_0_), channel_id=1, source_target_pairs={{0,2},{2,0},{4,6},{6,4},{8,10},{10,8},{12,14},{14,12},{16,18},{18,... | collective-permute-start | bytes 2359304 | tf_op jit(solution)/shard_map/ppermute | solution.py:921
  81.1 40.9 %collective-permute-start.13 = (bf16[2,1792,256]{2,1,0:T(8,128)(2,1)}, bf16[2,1792,256]{2,1,0:T(8,128)(2,1)S(1)}, u32[]{:S(2)}, u32[]{:S(2)}) collective-permute-start(bf16[2,1792,256]{2,1,0:T(8,128)(2,1)} %get-tuple-element.106), channel_id=1, source_target_pairs={{0,8},{2,10},{4,12},{6,14},{8,0},{10,2},{12,4},{14,6},{16,24},{18,... | collective-permute-start | bytes 5505032 | tf_op jit(solution)/shard_map/ppermute | solution.py:921
  81.3 27.6 %collective-permute-start.10 = (bf16[256,1536]{1,0:T(8,128)(2,1)S(1)}, bf16[256,1536]{1,0:T(8,128)(2,1)}, u32[]{:S(2)}, u32[]{:S(2)}) collective-permute-start(bf16[256,1536]{1,0:T(8,128)(2,1)S(1)} %collective-permute-done.6.refs_1_), channel_id=1, source_target_pairs={{0,2},{2,0},{4,6},{6,4},{8,10},{10,8},{12,14},{14,12},{16,18},{18,... | collective-permute-start | bytes 2359304 | tf_op jit(solution)/shard_map/ppermute | solution.py:921
  106.6 21.9 %collective-permute-start.12 = (bf16[2,896,256]{2,1,0:T(8,128)(2,1)S(1)}, bf16[2,896,256]{2,1,0:T(8,128)(2,1)S(1)}, u32[]{:S(2)}, u32[]{:S(2)}) collective-permute-start(bf16[2,896,256]{2,1,0:T(8,128)(2,1)S(1)} %bitcast.179), channel_id=1, source_target_pairs={{0,2},{2,0},{4,6},{6,4},{8,10},{10,8},{12,14},{14,12},{16,18},{18,... | collective-permute-start | bytes 2752520 | tf_op jit(solution)/shard_map/ppermute | solution.py:921
  107.8 20.6 %collective-permute-start.14 = (bf16[1792,256]{1,0:T(8,128)(2,1)S(1)}, bf16[1792,256]{1,0:T(8,128)(2,1)S(1)}, u32[]{:S(2)}, u32[]{:S(2)}) collective-permute-start(bf16[1792,256]{1,0:T(8,128)(2,1)S(1)} %broadcast_select_fusion), channel_id=1, source_target_pairs={{0,4},{2,6},{4,0},{6,2},{8,12},{10,14},{12,8},{14,10},{16,20},{18,... | collective-permute-start | bytes 2752520 | tf_op jit(solution)/shard_map/ppermute | solution.py:921
  136.7 23.5 %collective-permute-start.16 = (bf16[2,896,256]{2,1,0:T(8,128)(2,1)}, bf16[2,896,256]{2,1,0:T(8,128)(2,1)}, u32[]{:S(2)}, u32[]{:S(2)}) collective-permute-start(bf16[2,896,256]{2,1,0:T(8,128)(2,1)} %bitcast.21), channel_id=1, source_target_pairs={{0,2},{2,0},{4,6},{6,4},{8,10},{10,8},{12,14},{14,12},{16,18},{18,... | collective-permute-start | bytes 2752520 | tf_op jit(solution)/shard_map/ppermute | solution.py:921
  138.7 44.4 %collective-permute-start.23 = (bf16[256,1536]{1,0:T(8,128)(2,1)}, bf16[256,1536]{1,0:T(8,128)(2,1)}, u32[]{:S(2)}, u32[]{:S(2)}) collective-permute-start(bf16[256,1536]{1,0:T(8,128)(2,1)} %get-tuple-element.127.branch_own), channel_id=1, source_target_pairs={{0,2},{2,0},{4,6},{6,4},{8,10},{10,8},{12,14},{14,12},{16,18},{18,... | collective-permute-start | bytes 2359304 | tf_op jit(solution)/shard_map/ppermute | solution.py:921
  140.3 34.7 %collective-permute-start.17 = (bf16[384,512]{1,0:T(8,128)(2,1)S(1)}, bf16[384,512]{1,0:T(8,128)(2,1)}, u32[]{:S(2)}, u32[]{:S(2)}) collective-permute-start(bf16[384,512]{1,0:T(8,128)(2,1)S(1)} %copy-done.23), channel_id=1, source_target_pairs={{0,4},{2,6},{4,8},{6,10},{8,12},{10,14},{12,16},{14,18},{16,20},{1... | collective-permute-start | bytes 1179656 | tf_op jit(solution)/shard_map/ppermute | solution.py:927
  143.2 32.3 %collective-permute-start.18 = (bf16[384,512]{1,0:T(8,128)(2,1)}, bf16[384,512]{1,0:T(8,128)(2,1)}, u32[]{:S(2)}, u32[]{:S(2)}) collective-permute-start(bf16[384,512]{1,0:T(8,128)(2,1)} %get-tuple-element.116), channel_id=1, source_target_pairs={{4,0},{6,2},{8,4},{10,6},{12,8},{14,10},{16,12},{18,14},{20,16},{2... | collective-permute-start | bytes 1179656 | tf_op jit(solution)/shard_map/ppermute | solution.py:927
  145.4 26.9 %collective-permute-start.19 = (bf16[384,256]{1,0:T(8,128)(2,1)S(1)}, bf16[384,256]{1,0:T(8,128)(2,1)S(1)}, u32[]{:S(2)}, u32[]{:S(2)}) collective-permute-start(bf16[384,256]{1,0:T(8,128)(2,1)S(1)} %copy-done.29), channel_id=1, source_target_pairs={{0,8},{2,10},{4,12},{6,14},{8,16},{10,18},{12,20},{14,22},{16,24},... | collective-permute-start | bytes 589832 | tf_op jit(solution)/shard_map/ppermute | solution.py:927
  160.2 14.8 %collective-permute-start.20 = (bf16[384,256]{1,0:T(8,128)(2,1)S(1)}, bf16[384,256]{1,0:T(8,128)(2,1)S(1)}, u32[]{:S(2)}, u32[]{:S(2)}) collective-permute-start(bf16[384,256]{1,0:T(8,128)(2,1)S(1)} %copy-done.28), channel_id=1, source_target_pairs={{8,0},{10,2},{12,4},{14,6},{16,8},{18,10},{20,12},{22,14},{24,16},... | collective-permute-start | bytes 589832 | tf_op jit(solution)/shard_map/ppermute | solution.py:927
  172.3 46.0 %collective-permute-start.29 = (bf16[2,2,224,768]{3,2,1,0:T(8,128)(2,1)}, bf16[2,2,224,768]{3,2,1,0:T(8,128)(2,1)}, u32[]{:S(2)}, u32[]{:S(2)}) collective-permute-start(bf16[2,2,224,768]{3,2,1,0:T(8,128)(2,1)} %fusion), channel_id=1, source_target_pairs={{0,8},{2,10},{4,12},{6,14},{8,0},{10,2},{12,4},{14,6},{16,24},{18,... | collective-permute-start | bytes 4128776 | tf_op jit(solution)/shard_map/ppermute | solution.py:921
  175.0 14.1 %collective-permute-start.21 = (bf16[896,768]{1,0:T(8,128)(2,1)}, bf16[896,768]{1,0:T(8,128)(2,1)S(1)}, u32[]{:S(2)}, u32[]{:S(2)}) collective-permute-start(bf16[896,768]{1,0:T(8,128)(2,1)} %get-tuple-element.121), channel_id=1, source_target_pairs={{0,1},{1,0},{2,3},{3,2},{4,5},{5,4},{6,7},{7,6},{8,9},{9,8},{10,11... | collective-permute-start | bytes 4128776 | tf_op jit(solution)/shard_map/ppermute | solution.py:921
  178.6 12.9 %collective-permute-start.24 = (bf16[576,256]{1,0:T(8,128)(2,1)}, bf16[576,256]{1,0:T(8,128)(2,1)S(1)}, u32[]{:S(2)}, u32[]{:S(2)}) collective-permute-start(bf16[576,256]{1,0:T(8,128)(2,1)} %get-tuple-element.131), channel_id=1, source_target_pairs={{0,2},{2,0},{4,6},{6,4},{8,10},{10,8},{12,14},{14,12},{16,18},{18,... | collective-permute-start | bytes 884744 | tf_op jit(solution)/shard_map/ppermute | solution.py:921
  182.3 18.7 %collective-permute-start.26 = (bf16[2,224,768]{2,1,0:T(8,128)(2,1)}, bf16[2,224,768]{2,1,0:T(8,128)(2,1)}, u32[]{:S(2)}, u32[]{:S(2)}) collective-permute-start(bf16[2,224,768]{2,1,0:T(8,128)(2,1)} %get-tuple-element.179), channel_id=1, source_target_pairs={{0,4},{2,6},{4,0},{6,2},{8,12},{10,14},{12,8},{14,10},{16,20},{18,... | collective-permute-start | bytes 2064392 | tf_op jit(solution)/shard_map/ppermute | solution.py:921
  190.4 23.9 %collective-permute-start.30 = (bf16[2,224,768]{2,1,0:T(8,128)(2,1)}, bf16[2,224,768]{2,1,0:T(8,128)(2,1)}, u32[]{:S(2)}, u32[]{:S(2)}) collective-permute-start(bf16[2,224,768]{2,1,0:T(8,128)(2,1)} %get-tuple-element.177), channel_id=1, source_target_pairs={{0,4},{2,6},{4,0},{6,2},{8,12},{10,14},{12,8},{14,10},{16,20},{18,... | collective-permute-start | bytes 2064392 | tf_op jit(solution)/shard_map/ppermute | solution.py:921
  191.5 30.1 %collective-permute-start.28 = (bf16[768,768]{1,0:T(8,128)(2,1)}, bf16[768,768]{1,0:T(8,128)(2,1)}, u32[]{:S(2)}, u32[]{:S(2)}) collective-permute-start(bf16[768,768]{1,0:T(8,128)(2,1)} %get-tuple-element.139), channel_id=1, source_target_pairs={{0,1},{1,0},{2,3},{3,2},{4,5},{5,4},{6,7},{7,6},{8,9},{9,8},{10,11... | collective-permute-start | bytes 3538952 | tf_op jit(solution)/shard_map/ppermute | solution.py:921
  202.2 50.2 %collective-permute-start.40 = (bf16[224,768]{1,0:T(8,128)(2,1)S(1)}, bf16[224,768]{1,0:T(8,128)(2,1)S(1)}, u32[]{:S(2)}, u32[]{:S(2)}) collective-permute-start(bf16[224,768]{1,0:T(8,128)(2,1)S(1)} %get-tuple-element.183), channel_id=1, source_target_pairs={{0,16},{2,18},{4,20},{6,22},{8,24},{10,26},{12,28},{14,30},{16,0},... | collective-permute-start | bytes 1032200 | tf_op jit(solution)/shard_map/ppermute | solution.py:921
  215.5 20.7 %collective-permute-start.41 = (bf16[224,768]{1,0:T(8,128)(2,1)S(1)}, bf16[224,768]{1,0:T(8,128)(2,1)S(1)}, u32[]{:S(2)}, u32[]{:S(2)}) collective-permute-start(bf16[224,768]{1,0:T(8,128)(2,1)S(1)} %get-tuple-element.185), channel_id=1, source_target_pairs={{0,16},{2,18},{4,20},{6,22},{8,24},{10,26},{12,28},{14,30},{16,0},... | collective-permute-start | bytes 1032200 | tf_op jit(solution)/shard_map/ppermute | solution.py:921
  219.9 15.8 %collective-permute-start.34 = (bf16[2,224,768]{2,1,0:T(8,128)(2,1)S(1)}, bf16[2,224,768]{2,1,0:T(8,128)(2,1)S(1)}, u32[]{:S(2)}, u32[]{:S(2)}) collective-permute-start(bf16[2,224,768]{2,1,0:T(8,128)(2,1)S(1)} %get-tuple-element.175), channel_id=1, source_target_pairs={{0,2},{2,0},{4,6},{6,4},{8,10},{10,8},{12,14},{14,12},{16,18},{18,... | collective-permute-start | bytes 2064392 | tf_op jit(solution)/shard_map/ppermute | solution.py:921
  221.3 14.9 %collective-permute-start.27 = (f32[25,128]{1,0:T(8,128)S(1)}, f32[25,128]{1,0:T(8,128)S(1)}, u32[]{:S(2)}, u32[]{:S(2)}) collective-permute-start(f32[25,128]{1,0:T(8,128)S(1)} %fusion.43), channel_id=1, source_target_pairs={{0,4},{2,6},{4,0},{6,2},{8,12},{10,14},{12,8},{14,10},{16,20},{18,... | collective-permute-start | bytes 38408 | tf_op jit(solution)/shard_map/ppermute | solution.py:921
  224.3 27.8 %collective-permute-start.33 = (bf16[2,2,96,768]{3,2,1,0:T(8,128)(2,1)S(1)}, bf16[2,2,96,768]{3,2,1,0:T(8,128)(2,1)S(1)}, u32[]{:S(2)}, u32[]{:S(2)}) collective-permute-start(bf16[2,2,96,768]{3,2,1,0:T(8,128)(2,1)S(1)} %copy.57), channel_id=1, source_target_pairs={{0,4},{2,6},{4,0},{6,2},{8,12},{10,14},{12,8},{14,10},{16,20},{18,... | collective-permute-start | bytes 1769480 | tf_op jit(solution)/shard_map/ppermute | solution.py:921
  235.8 15.5 %collective-permute-start.42 = (bf16[224,768]{1,0:T(8,128)(2,1)S(1)}, bf16[224,768]{1,0:T(8,128)(2,1)S(1)}, u32[]{:S(2)}, u32[]{:S(2)}) collective-permute-start(bf16[224,768]{1,0:T(8,128)(2,1)S(1)} %fusion.20), channel_id=1, source_target_pairs={{0,16},{2,18},{4,20},{6,22},{8,24},{10,26},{12,28},{14,30},{16,0},... | collective-permute-start | bytes 1032200 | tf_op jit(solution)/shard_map/ppermute | solution.py:921
  236.3 16.2 %collective-permute-start.31 = (f32[25,128]{1,0:T(8,128)S(1)}, f32[25,128]{1,0:T(8,128)S(1)}, u32[]{:S(2)}, u32[]{:S(2)}) collective-permute-start(f32[25,128]{1,0:T(8,128)S(1)} %fusion.48), channel_id=1, source_target_pairs={{0,2},{2,0},{4,6},{6,4},{8,10},{10,8},{12,14},{14,12},{16,18},{18,... | collective-permute-start | bytes 38408 | tf_op jit(solution)/shard_map/ppermute | solution.py:921
  251.4 21.2 %collective-permute-start.43 = (bf16[224,768]{1,0:T(8,128)(2,1)S(1)}, bf16[224,768]{1,0:T(8,128)(2,1)S(1)}, u32[]{:S(2)}, u32[]{:S(2)}) collective-permute-start(bf16[224,768]{1,0:T(8,128)(2,1)S(1)} %fusion.6), channel_id=1, source_target_pairs={{0,0},{2,2},{4,16},{6,18},{8,8},{10,10},{12,24},{14,26},{16,4},{18... | collective-permute-start | bytes 1032200 | tf_op jit(solution)/shard_map/ppermute | solution.py:1219
  252.3 17.5 %collective-permute-start.36 = (bf16[2,96,768]{2,1,0:T(8,128)(2,1)S(1)}, bf16[2,96,768]{2,1,0:T(8,128)(2,1)S(1)}, u32[]{:S(2)}, u32[]{:S(2)}) collective-permute-start(bf16[2,96,768]{2,1,0:T(8,128)(2,1)S(1)} %get-tuple-element.187), channel_id=1, source_target_pairs={{0,8},{2,10},{4,12},{6,14},{8,0},{10,2},{12,4},{14,6},{16,24},{18,... | collective-permute-start | bytes 884744 | tf_op jit(solution)/shard_map/ppermute | solution.py:921
  262.3 10.3 %collective-permute-start.35 = (f32[25,128]{1,0:T(8,128)S(1)}, f32[25,128]{1,0:T(8,128)S(1)}, u32[]{:S(2)}, u32[]{:S(2)}) collective-permute-start(f32[25,128]{1,0:T(8,128)S(1)} %add.318), channel_id=1, source_target_pairs={{0,16},{2,18},{4,20},{6,22},{8,24},{10,26},{12,28},{14,30},{16,0},... | collective-permute-start | bytes 38408 | tf_op jit(solution)/shard_map/ppermute | solution.py:921
  (48 other events, 333.3 us)
